TPU v7x, 32 devices: a whole 2x2x4 slice. The times are simulated.
32 devices in a mesh: head: 4 (over y, x), seq: 8 (over z, core).
Axes of the slice: x: 2, y: 2, z: 4, core: 2. Of those that a mesh axis runs over, the one named last changes fastest.
Arguments:
- seq_input: bfloat16 [8192, 8192], P('seq', 'head'), may hold values from -6 to 6
- step_size: float32 [128, 8192], P('head', 'seq'), may hold values from 0.25 to 2
- decay_rate: float32 [128], P('head'), may hold values from 0 to 0.03, as said below
- skip_gain: float32 [128], P('head'), may hold values from 0.5 to 1.5
- state_write: bfloat16 [8192, 1024], P('seq', 'head'), may hold values from -0.44921875 to 0.44921875
- state_read: bfloat16 [8192, 1024], P('seq', 'head'), may hold values from -0.44921875 to 0.44921875
- out_grad: bfloat16 [8192, 8192], P('seq', 'head'), may hold values from -1.5 to 1.5
- segment_order: int32 [8], replicated, may hold values from 0 to 7, each once
- doc_start: int32 [32], replicated, may hold values from 0 to 256, as said below
Outputs:
- mixed_out: bfloat16 [8192, 8192], P('seq', 'head')
- input_grad: bfloat16 [8192, 8192], P('seq', 'head')
- write_grad: float32 [8192, 1024], P('seq', 'head')
- read_grad: float32 [8192, 1024], P('seq', 'head')
Inputs may be any that keep to these rules, and one draw needn't show every extreme that they name: Shard k along seq holds sequence segment segment_order[k]; every segment once. A document starts at position doc_start[b] of stored block b, and 256 means that none starts in it; some block starts one at its first token and some block has none. `decay_rate`: positive.
All inputs are finite; a program needn't handle non-finite values.
Results may differ from a plain program's by a relative error of at most 0.0095.
Values may be sent and summed in bfloat16 or wider, within the bound.
A program may use at most 128 MiB of HBM per device.

v0:
```python
import functools

import jax
import jax.numpy as jnp
from jax import lax
from jax.experimental import pallas as pl
from jax.experimental.pallas import tpu as pltpu
from jax.sharding import PartitionSpec as P

HEADS = 128
HEAD_DIM = 64
STATE = 128
GROUPS = 8
BLOCK = 256
CHUNK = 256
EXTRA = 16
VMEM_LIMIT = 50 * 1024 * 1024

F32 = jnp.float32
BF16 = jnp.bfloat16


def partner(block, axis, bit):
    count = lax.axis_size(axis)
    route = []
    for low in range(count):
        high = low | 1 << bit
        if high != low and high < count:
            route += [(low, high), (high, low)]
    return lax.ppermute(block, axis, route)


def dot_nn(a, b):
    return lax.dot_general(a, b, (((1,), (0,)), ((), ())), preferred_element_type=F32)


def dot_nt(a, b):
    return lax.dot_general(a, b, (((1,), (1,)), ((), ())), preferred_element_type=F32)


def dot_tn(a, b):
    return lax.dot_general(a, b, (((0,), (0,)), ((), ())), preferred_element_type=F32)


def iota(shape, dim):
    return lax.broadcasted_iota(jnp.int32, shape, dim)


def head_spread(heads, first_head, width):
    row = iota((2 * heads, width), 0)
    row = jnp.where(row >= heads, row - heads, row)
    return (row == first_head + iota((2 * heads, width), 1) // HEAD_DIM).astype(F32).astype(BF16)


def token_weights(step, rate):
    heads, length = step.shape
    both = jnp.concatenate([step, step], axis=0)
    row, col = iota((length, length), 0), iota((length, length), 1)
    lower = (row >= col).astype(F32).astype(BF16)
    eye = (row == col).astype(F32).astype(BF16)
    high = both.astype(BF16)
    rest = both - high.astype(F32)
    mid = rest.astype(BF16)
    low = (rest - mid.astype(F32)).astype(BF16)
    cum = -rate * (dot_nt(lower, high) + dot_nt(lower, mid) + dot_nt(lower, low))
    cols = dot_nt(eye, high) + dot_nt(eye, mid) + dot_nt(eye, low)
    left = iota((length, 2 * heads), 1) < heads

    def halves(value):
        top = value.astype(BF16).astype(F32)
        return jnp.where(left, top, value - top).astype(BF16)

    return halves(jnp.exp(cum)), halves(cols * jnp.exp(-cum))


def summary_kernel(
    heads,
    blocks,
    doc_ref,
    x_ref,
    g_ref,
    step_ref,
    rate_ref,
    b_ref,
    c_ref,
    msg_ref,
    pre_ref,
    suf_ref,
    scale_ref,
    e_ref,
    f_ref,
):
    chunk = pl.program_id(0)

    @pl.when(chunk == 0)
    def _():
        for k in range(blocks):
            rows = pl.ds(k * BLOCK, BLOCK)
            e_ref[rows, :], f_ref[rows, :] = token_weights(step_ref[:, rows], rate_ref[...])

    spread = head_spread(heads, chunk * (CHUNK // HEAD_DIM), CHUNK)
    position = iota((BLOCK, STATE), 0)
    ends, reads, decays = [], [], []
    for k in range(blocks):
        rows = pl.ds(k * BLOCK, BLOCK)
        doc = doc_ref[k]
        e_wide = dot_nn(e_ref[rows, :], spread)
        f_wide = dot_nn(f_ref[rows, :], spread)
        grad_in = (e_wide * g_ref[rows, :].astype(F32)).astype(BF16)
        data_in = (f_wide * x_ref[rows, :].astype(F32)).astype(BF16)
        write = jnp.where(position >= doc, b_ref[rows, :].astype(F32), 0.0).astype(BF16)
        read = jnp.where(position < doc, c_ref[rows, :].astype(F32), 0.0).astype(BF16)
        last = e_wide[BLOCK - 1 : BLOCK, :]
        ends.append(last * dot_tn(write, data_in))
        reads.append(dot_tn(read, grad_in))
        decays.append(jnp.where(doc == BLOCK, last, 0.0))
    state = jnp.zeros((STATE, CHUNK), F32)
    lead = jnp.ones((1, CHUNK), F32)
    for k in range(blocks):
        pre_ref[k] = state.astype(BF16)
        scale_ref[k : k + 1, :] = lead
        state = decays[k] * state + ends[k]
        lead = lead * decays[k]
    grad = jnp.zeros((STATE, CHUNK), F32)
    tail = jnp.ones((1, CHUNK), F32)
    for k in reversed(range(blocks)):
        suf_ref[k] = grad.astype(BF16)
        scale_ref[blocks + k : blocks + k + 1, :] = tail
        grad = reads[k] + decays[k] * grad
        tail = tail * decays[k]
    msg_ref[0, :STATE, :] = state.astype(BF16)
    msg_ref[0, STATE : 2 * STATE, :] = grad.astype(BF16)
    top = jnp.broadcast_to(lead, (EXTRA, CHUNK)).astype(BF16).astype(F32)
    rest = jnp.broadcast_to(lead, (EXTRA, CHUNK)) - top
    msg_ref[0, 2 * STATE :, :] = jnp.where(iota((EXTRA, CHUNK), 0) == 0, top, rest).astype(BF16)


def chain_kernel(count, order_ref, got_ref, out_ref):
    width = got_ref.shape[-1]

    def decay_of(shard):
        pair = got_ref[shard, 2 * STATE :, :].astype(F32)
        return pair[0:1, :] + pair[1:2, :]

    def forward(place, state):
        shard = order_ref[place]
        out_ref[shard, :STATE, :] = state.astype(BF16)
        return decay_of(shard) * state + got_ref[shard, :STATE, :].astype(F32)

    def backward(step, grad):
        shard = order_ref[count - 1 - step]
        out_ref[shard, STATE:, :] = grad.astype(BF16)
        return decay_of(shard) * grad + got_ref[shard, STATE : 2 * STATE, :].astype(F32)

    empty = jnp.zeros((STATE, width), F32)
    lax.fori_loop(0, count, forward, empty)
    lax.fori_loop(0, count, backward, empty)


def finish_kernel(
    heads,
    blocks,
    span,
    doc_ref,
    x_ref,
    g_ref,
    b_ref,
    c_ref,
    e_ref,
    f_ref,
    pre_ref,
    suf_ref,
    scale_ref,
    dev_ref,
    skip_ref,
    y_ref,
    dx_ref,
    dw_ref,
    dr_ref,
):
    group, k = pl.program_id(0), pl.program_id(1)
    doc = doc_ref[k]
    width = span * HEAD_DIM
    spread = head_spread(heads, group * span, width)
    e_wide = dot_nn(e_ref[...], spread)
    f_wide = dot_nn(f_ref[...], spread)
    x = x_ref[...].astype(F32)
    g = g_ref[...].astype(F32)
    grad_in = (e_wide * g).astype(BF16)
    data_in = (f_wide * x).astype(BF16)
    position = iota((BLOCK, STATE), 0)
    b, c = b_ref[...], c_ref[...]
    write_on, read_on = position >= doc, position < doc
    write = jnp.where(write_on, b.astype(F32), 0.0).astype(BF16)
    read = jnp.where(read_on, c.astype(F32), 0.0).astype(BF16)
    state_dev = jnp.concatenate([dev_ref[j, :STATE, :] for j in range(dev_ref.shape[0])], axis=1)
    grad_dev = jnp.concatenate([dev_ref[j, STATE:, :] for j in range(dev_ref.shape[0])], axis=1)
    scales = scale_ref[...]
    which = iota(scales.shape, 0)
    lead = jnp.sum(jnp.where(which == k, scales, 0.0), axis=0, keepdims=True)
    tail = jnp.sum(jnp.where(which == blocks + k, scales, 0.0), axis=0, keepdims=True)
    last = e_wide[BLOCK - 1 : BLOCK, :]
    state = (pre_ref[0].astype(F32) + lead * state_dev.astype(F32)).astype(BF16)
    grad = (last * (suf_ref[0].astype(F32) + tail * grad_dev.astype(F32))).astype(BF16)
    row, col = iota((BLOCK, BLOCK), 0), iota((BLOCK, BLOCK), 1)
    keep = (row >= col) & ((row < doc) | (col >= doc))
    keep_t = (col >= row) & ((col < doc) | (row >= doc))
    score = jnp.where(keep, dot_nt(c, b), 0.0).astype(BF16)
    score_t = jnp.where(keep_t, dot_nt(b, c), 0.0).astype(BF16)
    skip = skip_ref[...]
    y_ref[...] = (e_wide * (dot_nn(score, data_in) + dot_nn(read, state)) + skip * x).astype(BF16)
    dx_ref[...] = (f_wide * (dot_nn(score_t, grad_in) + dot_nn(write, grad)) + skip * g).astype(
        BF16
    )
    score_grad = jnp.where(keep, dot_nt(grad_in, data_in), 0.0).astype(BF16)
    dw_ref[...] = dot_tn(score_grad, c) + jnp.where(write_on, dot_nt(data_in, grad), 0.0)
    dr_ref[...] = dot_nn(score_grad, b) + jnp.where(read_on, dot_nt(grad_in, state), 0.0)


def on_device(
    seq_input,
    step_size,
    decay_rate,
    skip_gain,
    state_write,
    state_read,
    out_grad,
    segment_order,
    doc_start,
):
    heads = decay_rate.shape[0]
    group_heads = HEADS // GROUPS
    span = min(heads, group_heads)
    groups = heads // span
    group_devices = max(1, group_heads // heads)
    levels = group_devices.bit_length() - 1
    tokens = seq_input.shape[0]
    blocks = tokens // BLOCK
    channels = heads * HEAD_DIM
    chunks = channels // CHUNK
    group_chunks = chunks // groups
    seq_count = lax.axis_size("seq")
    head_rank = lax.axis_index("head")
    seq_rank = lax.axis_index("seq")
    own_write, own_read = (state_write, state_read)
    for level in range(levels):
        other_write, other_read = partner((own_write, own_read), "head", level)
        upper_half = head_rank >> level & 1 == 1
        own_write = jnp.where(
            upper_half,
            jnp.concatenate([other_write, own_write], 1),
            jnp.concatenate([own_write, other_write], 1),
        )
        own_read = jnp.where(
            upper_half,
            jnp.concatenate([other_read, own_read], 1),
            jnp.concatenate([own_read, other_read], 1),
        )
    doc_here = lax.dynamic_slice_in_dim(doc_start, seq_rank * blocks, blocks)
    rate_row = jnp.concatenate([decay_rate, decay_rate]).reshape(1, 2 * heads)
    skip_row = jnp.repeat(skip_gain, HEAD_DIM).reshape(1, channels)
    smem = pl.BlockSpec(memory_space=pltpu.SMEM)
    params = pltpu.CompilerParams(vmem_limit_bytes=VMEM_LIMIT)
    rows = 2 * STATE + EXTRA

    message, pre, suf, scales, e_cols, f_cols = pl.pallas_call(
        functools.partial(summary_kernel, heads, blocks),
        grid=(chunks,),
        out_shape=(
            jax.ShapeDtypeStruct((chunks, rows, CHUNK), BF16),
            jax.ShapeDtypeStruct((blocks, STATE, channels), BF16),
            jax.ShapeDtypeStruct((blocks, STATE, channels), BF16),
            jax.ShapeDtypeStruct((2 * blocks, channels), F32),
            jax.ShapeDtypeStruct((tokens, 2 * heads), BF16),
            jax.ShapeDtypeStruct((tokens, 2 * heads), BF16),
        ),
        in_specs=[
            smem,
            pl.BlockSpec((tokens, CHUNK), lambda i: (0, i)),
            pl.BlockSpec((tokens, CHUNK), lambda i: (0, i)),
            pl.BlockSpec((heads, tokens), lambda i: (0, 0)),
            pl.BlockSpec((1, 2 * heads), lambda i: (0, 0)),
            pl.BlockSpec((tokens, STATE), lambda i: (0, i // group_chunks)),
            pl.BlockSpec((tokens, STATE), lambda i: (0, i // group_chunks)),
        ],
        out_specs=(
            pl.BlockSpec((1, rows, CHUNK), lambda i: (i, 0, 0)),
            pl.BlockSpec((blocks, STATE, CHUNK), lambda i: (0, 0, i)),
            pl.BlockSpec((blocks, STATE, CHUNK), lambda i: (0, 0, i)),
            pl.BlockSpec((2 * blocks, CHUNK), lambda i: (0, i)),
            pl.BlockSpec((tokens, 2 * heads), lambda i: (0, 0)),
            pl.BlockSpec((tokens, 2 * heads), lambda i: (0, 0)),
        ),
        compiler_params=params,
        name="summary",
    )(doc_here, seq_input, out_grad, step_size, rate_row, own_write, own_read)

    width = channels // seq_count
    direct = chunks == seq_count
    if not direct:
        message = jnp.transpose(message, (1, 0, 2)).reshape(rows, seq_count, width)
        message = jnp.transpose(message, (1, 0, 2))
    got = lax.all_to_all(message, "seq", split_axis=0, concat_axis=0, tiled=True)
    order = jnp.zeros((seq_count,), jnp.int32).at[segment_order].set(
        jnp.arange(seq_count, dtype=jnp.int32)
    )
    answer = pl.pallas_call(
        functools.partial(chain_kernel, seq_count),
        out_shape=jax.ShapeDtypeStruct((seq_count, 2 * STATE, width), BF16),
        in_specs=[smem, pl.BlockSpec(memory_space=pltpu.VMEM)],
        out_specs=pl.BlockSpec(memory_space=pltpu.VMEM),
        compiler_params=params,
        name="chain",
    )(order, got)
    device = lax.all_to_all(answer, "seq", split_axis=0, concat_axis=0, tiled=True)
    if not direct:
        device = jnp.transpose(device, (1, 0, 2)).reshape(2 * STATE, chunks, CHUNK)
        device = jnp.transpose(device, (1, 0, 2))

    lanes = span * HEAD_DIM
    mixed, input_grad, write_sum, read_sum = pl.pallas_call(
        functools.partial(finish_kernel, heads, blocks, span),
        grid=(groups, blocks),
        out_shape=(
            jax.ShapeDtypeStruct((tokens, channels), BF16),
            jax.ShapeDtypeStruct((tokens, channels), BF16),
            jax.ShapeDtypeStruct((tokens, groups * STATE), F32),
            jax.ShapeDtypeStruct((tokens, groups * STATE), F32),
        ),
        in_specs=[
            smem,
            pl.BlockSpec((BLOCK, lanes), lambda g, k: (k, g)),
            pl.BlockSpec((BLOCK, lanes), lambda g, k: (k, g)),
            pl.BlockSpec((BLOCK, STATE), lambda g, k: (k, g)),
            pl.BlockSpec((BLOCK, STATE), lambda g, k: (k, g)),
            pl.BlockSpec((BLOCK, 2 * heads), lambda g, k: (k, 0)),
            pl.BlockSpec((BLOCK, 2 * heads), lambda g, k: (k, 0)),
            pl.BlockSpec((1, STATE, lanes), lambda g, k: (k, 0, g)),
            pl.BlockSpec((1, STATE, lanes), lambda g, k: (k, 0, g)),
            pl.BlockSpec((2 * blocks, lanes), lambda g, k: (0, g)),
            pl.BlockSpec((group_chunks, 2 * STATE, CHUNK), lambda g, k: (g, 0, 0)),
            pl.BlockSpec((1, lanes), lambda g, k: (0, g)),
        ],
        out_specs=(
            pl.BlockSpec((BLOCK, lanes), lambda g, k: (k, g)),
            pl.BlockSpec((BLOCK, lanes), lambda g, k: (k, g)),
            pl.BlockSpec((BLOCK, STATE), lambda g, k: (k, g)),
            pl.BlockSpec((BLOCK, STATE), lambda g, k: (k, g)),
        ),
        compiler_params=params,
        name="finish",
    )(
        doc_here,
        seq_input,
        out_grad,
        own_write,
        own_read,
        e_cols,
        f_cols,
        pre,
        suf,
        scales,
        device,
        skip_row,
    )

    for level in range(levels):
        other_write_sum, other_read_sum = partner(
            (write_sum.astype(BF16), read_sum.astype(BF16)), "head", level
        )
        write_sum = write_sum + other_write_sum.astype(F32)
        read_sum = read_sum + other_read_sum.astype(F32)
    own_width = groups * STATE // group_devices
    if group_devices > 1:
        own_first = head_rank % group_devices * own_width
        write_sum = lax.dynamic_slice_in_dim(write_sum, own_first, own_width, 1)
        read_sum = lax.dynamic_slice_in_dim(read_sum, own_first, own_width, 1)
    return mixed, input_grad, write_sum, read_sum


def solution(mesh):
    placed = (
        P("seq", "head"),
        P("head", "seq"),
        P("head"),
        P("head"),
        P("seq", "head"),
        P("seq", "head"),
        P("seq", "head"),
        P(),
        P(),
    )
    return jax.shard_map(
        on_device,
        mesh=mesh,
        in_specs=placed,
        out_specs=(P("seq", "head"), P("seq", "head"), P("seq", "head"), P("seq", "head")),
        check_vma=False,
    )
```

profile of v0, /device:TPU:0, one launch (start us, length us, event | category | flops | bytes accessed | tf_op | source)
XLA Modules:
  0.0 101.9 jit_solution(10791091746333203448)
XLA Ops:
  0.6 0.8 maximum_bitcast_fusion.rate_ref
  1.4 0.7 dynamic_slice.3.doc_ref
  2.2 0.0 copy-start
  2.2 1.0 %copy-done = bf16[1024,256]{1,0:T(8,128)(2,1)S(1)} copy-done((bf16[1024,256]{1,0:T(8,128)(2,1)S(1)}, bf16[1024,256]{1,0:T(8,128)(2,1)}, u32[]{:S(2)}) %copy-start) | copy-done | bytes 524312
  3.2 0.0 copy-start.2
  3.2 1.0 %copy-done.2 = bf16[1024,256]{1,0:T(8,128)(2,1)S(1)} copy-done((bf16[1024,256]{1,0:T(8,128)(2,1)S(1)}, bf16[1024,256]{1,0:T(8,128)(2,1)}, u32[]{:S(2)}) %copy-start.2) | copy-done | bytes 524312
  4.3 0.0 copy-start.4
  4.3 0.9 copy-done.4
  5.2 0.0 copy-start.6
  5.2 12.7 %summary.1 = (bf16[8,272,256]{2,1,0:T(8,128)(2,1)}, bf16[4,128,2048]{2,1,0:T(8,128)(2,1)}, bf16[4,128,2048]{2,1,0:T(8,128)(2,1)}, f32[8,2048]{1,0:T(8,128)S(1)},...) custom-call(s32[4]{0:T(128)S(1)} %dynamic_slice.3.doc_ref, bf16[1024,2048]{1,0:T(8,128)(2,1)} %x_ref.3, ...), custom_call_target="tpu_custom_call" | custom-call | tf_op jit(solution)/shard_map/summary/pallas_call | solution.py:266
  17.8 0.0 copy-start.5
  17.8 0.0 copy-start.1
  17.8 0.0 copy-start.3
  17.9 6.5 %all-to-all-start = ((bf16[8,272,256]{2,1,0:T(8,128)(2,1)}), bf16[8,272,256]{2,1,0:T(8,128)(2,1)S(1)}, u32[]{:S(2)}, u32[]{:S(2)}) async-start(bf16[8,272,256]{2,1,0:T(8,128)(2,1)} %get-tuple-element.15), calls=%async_computation | async-start | bytes 2228224 | tf_op jit(solution)/shard_map/all_to_all | solution.py:303
  24.3 0.0 copy-done.6
  24.4 0.6 scatter_custom_fusion.order_ref
  25.0 27.4 %all-to-all-done.got_ref = bf16[8,272,256]{2,1,0:T(8,128)(2,1)S(1)} async-done(((bf16[8,272,256]{2,1,0:T(8,128)(2,1)}), bf16[8,272,256]{2,1,0:T(8,128)(2,1)S(1)}, u32[]{:S(2)}, u32[]{:S(2)}) %all-to-all-start) | async-done | bytes 1114144 | tf_op jit(solution)/shard_map/all_to_all | solution.py:303
  52.3 1.9 %chain.1 = bf16[8,256,256]{2,1,0:T(8,128)(2,1)} custom-call(s32[8]{0:T(128)S(1)} %scatter_custom_fusion.order_ref, bf16[8,272,256]{2,1,0:T(8,128)(2,1)S(1)} %all-to-all-done.got_ref), custom_call_target="tpu_custom_call" | custom-call | tf_op jit(solution)/shard_map/chain/pallas_call | solution.py:307
  54.2 3.6 %all-to-all-start.1 = ((bf16[8,256,256]{2,1,0:T(8,128)(2,1)}), bf16[8,256,256]{2,1,0:T(8,128)(2,1)S(1)}, u32[]{:S(2)}, u32[]{:S(2)}) async-start(bf16[8,256,256]{2,1,0:T(8,128)(2,1)} %chain.1), calls=%async_computation.1 | async-start | bytes 2097152 | tf_op jit(solution)/shard_map/all_to_all | solution.py:315
  57.8 0.0 copy-done.5
  57.8 0.1 broadcast_in_dim.7
  57.9 0.1 reshape_reshape.3.skip_ref
  57.9 26.4 %all-to-all-done.1.dev_ref = bf16[8,256,256]{2,1,0:T(8,128)(2,1)S(1)} async-done(((bf16[8,256,256]{2,1,0:T(8,128)(2,1)}), bf16[8,256,256]{2,1,0:T(8,128)(2,1)S(1)}, u32[]{:S(2)}, u32[]{:S(2)}) %all-to-all-start.1) | async-done | bytes 1048608 | tf_op jit(solution)/shard_map/all_to_all | solution.py:315
  84.3 0.0 copy-done.1
  84.3 0.0 copy-done.3
  84.3 17.6 %finish.1 = (bf16[1024,2048]{1,0:T(8,128)(2,1)}, bf16[1024,2048]{1,0:T(8,128)(2,1)}, f32[1024,256]{1,0:T(8,128)}, f32[1024,256]{1,0:T(8,128)}) custom-call(s32[4]{0:T(128)S(1)} %dynamic_slice.3.doc_ref, bf16[1024,2048]{1,0:T(8,128)(2,1)} %x_ref.3, bf16[1024,2048]{1,0:T(8,128)(2,1)} %g_ref.3, bf16[1024,256]{1,0:T(8,128)(2,1)S(1)} %copy-done.1, ...), custom_call_target="tpu_custom_call" | custom-call | tf_op jit(solution)/shard_map/finish/pallas_call | solution.py:321
  (2 shorter events, 0.0 us)
Async XLA Ops:
  2.2 1.0 %copy-start = (bf16[1024,256]{1,0:T(8,128)(2,1)S(1)}, bf16[1024,256]{1,0:T(8,128)(2,1)}, u32[]{:S(2)}) copy-start(bf16[1024,256]{1,0:T(8,128)(2,1)} %b_ref.3) | copy-start | bytes 1572868
  3.2 1.0 %copy-start.2 = (bf16[1024,256]{1,0:T(8,128)(2,1)S(1)}, bf16[1024,256]{1,0:T(8,128)(2,1)}, u32[]{:S(2)}) copy-start(bf16[1024,256]{1,0:T(8,128)(2,1)} %c_ref.3) | copy-start | bytes 1572868
  4.3 0.9 copy-start.4
  5.2 19.2 %copy-start.6 = (s32[8]{0:T(128)S(1)}, s32[8]{0:T(128)}, u32[]{:S(2)}) copy-start(s32[8]{0:T(128)} %param.16) | copy-start | bytes 100
  17.8 39.9 %copy-start.5 = (f32[32]{0:T(128)S(1)}, f32[32]{0:T(128)}, u32[]{:S(2)}) copy-start(f32[32]{0:T(128)} %param.12) | copy-start | bytes 388
  17.8 66.5 %copy-start.1 = (bf16[1024,256]{1,0:T(8,128)(2,1)S(1)}, bf16[1024,256]{1,0:T(8,128)(2,1)}, u32[]{:S(2)}) copy-start(bf16[1024,256]{1,0:T(8,128)(2,1)} %b_ref.3) | copy-start | bytes 1572868
  17.8 66.4 %copy-start.3 = (bf16[1024,256]{1,0:T(8,128)(2,1)S(1)}, bf16[1024,256]{1,0:T(8,128)(2,1)}, u32[]{:S(2)}) copy-start(bf16[1024,256]{1,0:T(8,128)(2,1)} %c_ref.3) | copy-start | bytes 1572868
  17.9 34.5 %all-to-all-start = ((bf16[8,272,256]{2,1,0:T(8,128)(2,1)}), bf16[8,272,256]{2,1,0:T(8,128)(2,1)S(1)}, u32[]{:S(2)}, u32[]{:S(2)}) async-start(bf16[8,272,256]{2,1,0:T(8,128)(2,1)} %get-tuple-element.15), calls=%async_computation | async-start | bytes 2228224 | tf_op jit(solution)/shard_map/all_to_all | solution.py:303
  54.2 30.1 %all-to-all-start.1 = ((bf16[8,256,256]{2,1,0:T(8,128)(2,1)}), bf16[8,256,256]{2,1,0:T(8,128)(2,1)S(1)}, u32[]{:S(2)}, u32[]{:S(2)}) async-start(bf16[8,256,256]{2,1,0:T(8,128)(2,1)} %chain.1), calls=%async_computation.1 | async-start | bytes 2097152 | tf_op jit(solution)/shard_map/all_to_all | solution.py:315
where the time goes:
time: 102 us
  waiting for transfers between devices  53.7 us (53%)
  Pallas kernels  32.1 us (31%)
  starting transfers between devices  10 us (10%)
  local copies, waits for them, and re-layouts  4.49 us (4%)
    all_to_all x1, waiting for transfers between devices, on_device(): lax.all_to_all(message, 'seq', split_axis=0, concat_axis=0, tiled=True)  27.4 us
    all_to_all x1, waiting for transfers between devices, on_device(): lax.all_to_all(answer, 'seq', split_axis=0, concat_axis=0, tiled=True)  26.4 us
    pallas_call x1, Pallas kernels, on_device(): pl.pallas_call(functools.partial(finish_kernel, heads, blocks, span), gri...  17.6 us
    pallas_call x1, Pallas kernels, on_device(): pl.pallas_call(functools.partial(summary_kernel, heads, blocks), grid=(ch...  12.7 us
    all_to_all x1, starting transfers between devices, on_device(): lax.all_to_all(message, 'seq', split_axis=0, concat_axis=0, tiled=True)  6.48 us
    all_to_all x1, starting transfers between devices, on_device(): lax.all_to_all(answer, 'seq', split_axis=0, concat_axis=0, tiled=True)  3.56 us
    unnamed x14, local copies, waits for them, and re-layouts  3.01 us
  transfers between devices with their start and end apart: 2, of which 2 were waited for; matrix products, arithmetic and copies ran while one was open for 1% of the time, Pallas kernels for 0%

commit v1 on v0

--- a/solution.py
+++ b/solution.py
@@ -14,7 +14,7 @@
 BLOCK = 256
 CHUNK = 256
 EXTRA = 16
-VMEM_LIMIT = 50 * 1024 * 1024
+VMEM_LIMIT = 60 * 1024 * 1024
 
 F32 = jnp.float32
 BF16 = jnp.bfloat16
@@ -73,9 +73,15 @@
     return halves(jnp.exp(cum)), halves(cols * jnp.exp(-cum))
 
 
+def owner_at(step, count):
+    return lax.rem(step, 2) * (count // 2) + step // 2
+
+
 def summary_kernel(
     heads,
     blocks,
+    chunk,
+    first,
     doc_ref,
     x_ref,
     g_ref,
@@ -84,15 +90,14 @@
     b_ref,
     c_ref,
     msg_ref,
+    slot,
     pre_ref,
     suf_ref,
     scale_ref,
     e_ref,
     f_ref,
 ):
-    chunk = pl.program_id(0)
-
-    @pl.when(chunk == 0)
+    @pl.when(first)
     def _():
         for k in range(blocks):
             rows = pl.ds(k * BLOCK, BLOCK)
@@ -128,11 +133,17 @@
         scale_ref[blocks + k : blocks + k + 1, :] = tail
         grad = reads[k] + decays[k] * grad
         tail = tail * decays[k]
-    msg_ref[0, :STATE, :] = state.astype(BF16)
-    msg_ref[0, STATE : 2 * STATE, :] = grad.astype(BF16)
+    msg_ref[slot, :STATE, :] = state.astype(BF16)
+    msg_ref[slot, STATE : 2 * STATE, :] = grad.astype(BF16)
     top = jnp.broadcast_to(lead, (EXTRA, CHUNK)).astype(BF16).astype(F32)
     rest = jnp.broadcast_to(lead, (EXTRA, CHUNK)) - top
-    msg_ref[0, 2 * STATE :, :] = jnp.where(iota((EXTRA, CHUNK), 0) == 0, top, rest).astype(BF16)
+    msg_ref[slot, 2 * STATE :, :] = jnp.where(iota((EXTRA, CHUNK), 0) == 0, top, rest).astype(BF16)
+
+
+def summary_call(heads, blocks, *refs):
+    chunk = pl.program_id(0)
+    msg_ref = refs[7]
+    summary_kernel(heads, blocks, chunk, chunk == 0, *refs[:7], msg_ref, 0, *refs[8:])
 
 
 def chain_kernel(count, order_ref, got_ref, out_ref):
@@ -155,6 +166,151 @@
     empty = jnp.zeros((STATE, width), F32)
     lax.fori_loop(0, count, forward, empty)
     lax.fori_loop(0, count, backward, empty)
+
+
+def exchange_kernel(
+    heads,
+    blocks,
+    count,
+    doc_ref,
+    order_ref,
+    place_ref,
+    x_ref,
+    g_ref,
+    step_ref,
+    rate_ref,
+    b_ref,
+    c_ref,
+    pre_ref,
+    suf_ref,
+    scale_ref,
+    e_ref,
+    f_ref,
+    dev_ref,
+    msg,
+    got,
+    chain,
+    answer,
+    back,
+    send_sem,
+    recv_sem,
+    back_send_sem,
+    back_recv_sem,
+):
+    step = pl.program_id(0)
+    me = lax.axis_index("seq")
+    barrier = pltpu.get_barrier_semaphore()
+
+    def outward(owner, source):
+        return pltpu.make_async_remote_copy(
+            src_ref=msg.at[owner],
+            dst_ref=got.at[source],
+            send_sem=send_sem.at[owner],
+            recv_sem=recv_sem.at[source],
+            device_id={"seq": owner},
+            device_id_type=pl.DeviceIdType.MESH,
+        )
+
+    def homeward(shard, source):
+        return pltpu.make_async_remote_copy(
+            src_ref=answer.at[shard],
+            dst_ref=back.at[source],
+            send_sem=back_send_sem.at[shard],
+            recv_sem=back_recv_sem.at[source],
+            device_id={"seq": shard},
+            device_id_type=pl.DeviceIdType.MESH,
+        )
+
+    @pl.when(step == 0)
+    def _():
+        for ahead in range(1, count):
+            pl.semaphore_signal(
+                barrier,
+                inc=1,
+                device_id={"seq": lax.rem(me + ahead, count)},
+                device_id_type=pl.DeviceIdType.MESH,
+            )
+
+    @pl.when(step < count)
+    def _():
+        owner = owner_at(step, count)
+        summary_kernel(
+            heads,
+            blocks,
+            owner,
+            step == 0,
+            doc_ref,
+            x_ref,
+            g_ref,
+            step_ref,
+            rate_ref,
+            b_ref,
+            c_ref,
+            msg,
+            owner,
+            pre_ref,
+            suf_ref,
+            scale_ref,
+            e_ref,
+            f_ref,
+        )
+
+        @pl.when(step == 0)
+        def _():
+            pl.semaphore_wait(barrier, count - 1)
+
+        @pl.when(owner != me)
+        def _():
+            outward(owner, me).start()
+
+        @pl.when(owner == me)
+        def _():
+            got[me] = msg[owner]
+
+    @pl.when(step == count)
+    def _():
+        for shard in range(count):
+
+            @pl.when(me != shard)
+            def _():
+                outward(shard, shard).wait_recv()
+
+        def decay_of(shard):
+            pair = got[shard, 2 * STATE :, :].astype(F32)
+            return pair[0:1, :] + pair[1:2, :]
+
+        state = jnp.zeros((STATE, CHUNK), F32)
+        for place in range(count):
+            shard = order_ref[place]
+            chain[place, :STATE, :] = state.astype(BF16)
+            state = decay_of(shard) * state + got[shard, :STATE, :].astype(F32)
+        grad = jnp.zeros((STATE, CHUNK), F32)
+        for place in reversed(range(count)):
+            shard = order_ref[place]
+            chain[place, STATE:, :] = grad.astype(BF16)
+            grad = decay_of(shard) * grad + got[shard, STATE : 2 * STATE, :].astype(F32)
+        for shard in range(count):
+            answer[shard] = chain[place_ref[shard]]
+
+            @pl.when(me != shard)
+            def _():
+                homeward(shard, me).start()
+
+        back[me] = answer[me]
+        for shard in range(count):
+
+            @pl.when(me != shard)
+            def _():
+                homeward(shard, shard).wait_recv()
+
+        for shard in range(count):
+
+            @pl.when(me != shard)
+            def _():
+                outward(shard, me).wait_send()
+                homeward(shard, me).wait_send()
+
+        dev_ref[...] = back[...]
 
 
 def finish_kernel(
@@ -263,57 +419,116 @@
     params = pltpu.CompilerParams(vmem_limit_bytes=VMEM_LIMIT)
     rows = 2 * STATE + EXTRA
 
-    message, pre, suf, scales, e_cols, f_cols = pl.pallas_call(
-        functools.partial(summary_kernel, heads, blocks),
-        grid=(chunks,),
-        out_shape=(
-            jax.ShapeDtypeStruct((chunks, rows, CHUNK), BF16),
-            jax.ShapeDtypeStruct((blocks, STATE, channels), BF16),
-            jax.ShapeDtypeStruct((blocks, STATE, channels), BF16),
-            jax.ShapeDtypeStruct((2 * blocks, channels), F32),
-            jax.ShapeDtypeStruct((tokens, 2 * heads), BF16),
-            jax.ShapeDtypeStruct((tokens, 2 * heads), BF16),
-        ),
-        in_specs=[
-            smem,
-            pl.BlockSpec((tokens, CHUNK), lambda i: (0, i)),
-            pl.BlockSpec((tokens, CHUNK), lambda i: (0, i)),
-            pl.BlockSpec((heads, tokens), lambda i: (0, 0)),
-            pl.BlockSpec((1, 2 * heads), lambda i: (0, 0)),
-            pl.BlockSpec((tokens, STATE), lambda i: (0, i // group_chunks)),
-            pl.BlockSpec((tokens, STATE), lambda i: (0, i // group_chunks)),
-        ],
-        out_specs=(
-            pl.BlockSpec((1, rows, CHUNK), lambda i: (i, 0, 0)),
-            pl.BlockSpec((blocks, STATE, CHUNK), lambda i: (0, 0, i)),
-            pl.BlockSpec((blocks, STATE, CHUNK), lambda i: (0, 0, i)),
-            pl.BlockSpec((2 * blocks, CHUNK), lambda i: (0, i)),
-            pl.BlockSpec((tokens, 2 * heads), lambda i: (0, 0)),
-            pl.BlockSpec((tokens, 2 * heads), lambda i: (0, 0)),
-        ),
-        compiler_params=params,
-        name="summary",
-    )(doc_here, seq_input, out_grad, step_size, rate_row, own_write, own_read)
-
-    width = channels // seq_count
-    direct = chunks == seq_count
-    if not direct:
-        message = jnp.transpose(message, (1, 0, 2)).reshape(rows, seq_count, width)
-        message = jnp.transpose(message, (1, 0, 2))
-    got = lax.all_to_all(message, "seq", split_axis=0, concat_axis=0, tiled=True)
     order = jnp.zeros((seq_count,), jnp.int32).at[segment_order].set(
         jnp.arange(seq_count, dtype=jnp.int32)
     )
-    answer = pl.pallas_call(
-        functools.partial(chain_kernel, seq_count),
-        out_shape=jax.ShapeDtypeStruct((seq_count, 2 * STATE, width), BF16),
-        in_specs=[smem, pl.BlockSpec(memory_space=pltpu.VMEM)],
-        out_specs=pl.BlockSpec(memory_space=pltpu.VMEM),
-        compiler_params=params,
-        name="chain",
-    )(order, got)
-    device = lax.all_to_all(answer, "seq", split_axis=0, concat_axis=0, tiled=True)
-    if not direct:
+    if chunks == seq_count:
+
+        def served(i):
+            return owner_at(jnp.minimum(i, chunks - 1), chunks)
+
+        pre, suf, scales, e_cols, f_cols, device = pl.pallas_call(
+            functools.partial(exchange_kernel, heads, blocks, seq_count),
+            grid=(chunks + 1,),
+            out_shape=(
+                jax.ShapeDtypeStruct((blocks, STATE, channels), BF16),
+                jax.ShapeDtypeStruct((blocks, STATE, channels), BF16),
+                jax.ShapeDtypeStruct((2 * blocks, channels), F32),
+                jax.ShapeDtypeStruct((tokens, 2 * heads), BF16),
+                jax.ShapeDtypeStruct((tokens, 2 * heads), BF16),
+                jax.ShapeDtypeStruct((chunks, 2 * STATE, CHUNK), BF16),
+            ),
+            in_specs=[
+                smem,
+                smem,
+                smem,
+                pl.BlockSpec((tokens, CHUNK), lambda i: (0, served(i))),
+                pl.BlockSpec((tokens, CHUNK), lambda i: (0, served(i))),
+                pl.BlockSpec((heads, tokens), lambda i: (0, 0)),
+                pl.BlockSpec((1, 2 * heads), lambda i: (0, 0)),
+                pl.BlockSpec((tokens, STATE), lambda i: (0, served(i) // group_chunks)),
+                pl.BlockSpec((tokens, STATE), lambda i: (0, served(i) // group_chunks)),
+            ],
+            out_specs=(
+                pl.BlockSpec((blocks, STATE, CHUNK), lambda i: (0, 0, served(i))),
+                pl.BlockSpec((blocks, STATE, CHUNK), lambda i: (0, 0, served(i))),
+                pl.BlockSpec((2 * blocks, CHUNK), lambda i: (0, served(i))),
+                pl.BlockSpec((tokens, 2 * heads), lambda i: (0, 0)),
+                pl.BlockSpec((tokens, 2 * heads), lambda i: (0, 0)),
+                pl.BlockSpec((chunks, 2 * STATE, CHUNK), lambda i: (0, 0, 0)),
+            ),
+            scratch_shapes=[
+                pltpu.VMEM((chunks, rows, CHUNK), BF16),
+                pltpu.VMEM((chunks, rows, CHUNK), BF16),
+                pltpu.VMEM((chunks, 2 * STATE, CHUNK), BF16),
+                pltpu.VMEM((chunks, 2 * STATE, CHUNK), BF16),
+                pltpu.VMEM((chunks, 2 * STATE, CHUNK), BF16),
+                pltpu.SemaphoreType.DMA((chunks,)),
+                pltpu.SemaphoreType.DMA((chunks,)),
+                pltpu.SemaphoreType.DMA((chunks,)),
+                pltpu.SemaphoreType.DMA((chunks,)),
+            ],
+            compiler_params=pltpu.CompilerParams(
+                vmem_limit_bytes=VMEM_LIMIT, collective_id=0, has_side_effects=True
+            ),
+            name="exchange",
+        )(
+            doc_here,
+            order,
+            segment_order,
+            seq_input,
+            out_grad,
+            step_size,
+            rate_row,
+            own_write,
+            own_read,
+        )
+    else:
+        message, pre, suf, scales, e_cols, f_cols = pl.pallas_call(
+            functools.partial(summary_call, heads, blocks),
+            grid=(chunks,),
+            out_shape=(
+                jax.ShapeDtypeStruct((chunks, rows, CHUNK), BF16),
+                jax.ShapeDtypeStruct((blocks, STATE, channels), BF16),
+                jax.ShapeDtypeStruct((blocks, STATE, channels), BF16),
+                jax.ShapeDtypeStruct((2 * blocks, channels), F32),
+                jax.ShapeDtypeStruct((tokens, 2 * heads), BF16),
+                jax.ShapeDtypeStruct((tokens, 2 * heads), BF16),
+            ),
+            in_specs=[
+                smem,
+                pl.BlockSpec((tokens, CHUNK), lambda i: (0, i)),
+                pl.BlockSpec((tokens, CHUNK), lambda i: (0, i)),
+                pl.BlockSpec((heads, tokens), lambda i: (0, 0)),
+                pl.BlockSpec((1, 2 * heads), lambda i: (0, 0)),
+                pl.BlockSpec((tokens, STATE), lambda i: (0, i // group_chunks)),
+                pl.BlockSpec((tokens, STATE), lambda i: (0, i // group_chunks)),
+            ],
+            out_specs=(
+                pl.BlockSpec((1, rows, CHUNK), lambda i: (i, 0, 0)),
+                pl.BlockSpec((blocks, STATE, CHUNK), lambda i: (0, 0, i)),
+                pl.BlockSpec((blocks, STATE, CHUNK), lambda i: (0, 0, i)),
+                pl.BlockSpec((2 * blocks, CHUNK), lambda i: (0, i)),
+                pl.BlockSpec((tokens, 2 * heads), lambda i: (0, 0)),
+                pl.BlockSpec((tokens, 2 * heads), lambda i: (0, 0)),
+            ),
+            compiler_params=params,
+            name="summary",
+        )(doc_here, seq_input, out_grad, step_size, rate_row, own_write, own_read)
+
+        width = channels // seq_count
+        message = jnp.transpose(message, (1, 0, 2)).reshape(rows, seq_count, width)
+        message = jnp.transpose(message, (1, 0, 2))
+        got = lax.all_to_all(message, "seq", split_axis=0, concat_axis=0, tiled=True)
+        answer = pl.pallas_call(
+            functools.partial(chain_kernel, seq_count),
+            out_shape=jax.ShapeDtypeStruct((seq_count, 2 * STATE, width), BF16),
+            in_specs=[smem, pl.BlockSpec(memory_space=pltpu.VMEM)],
+            out_specs=pl.BlockSpec(memory_space=pltpu.VMEM),
+            compiler_params=params,
+            name="chain",
+        )(order, got)
+        device = lax.all_to_all(answer, "seq", split_axis=0, concat_axis=0, tiled=True)
         device = jnp.transpose(device, (1, 0, 2)).reshape(2 * STATE, chunks, CHUNK)
         device = jnp.transpose(device, (1, 0, 2))
 

time: 102 us -> 79.7 us (0.78)
  the two profiles are of different devices: /device:TPU:0 before, /device:TPU:29 now
where the time goes in v1:
time: 79.7 us; the launch traced here: 79.3 us
  Pallas kernels  72.9 us (91%)
  local copies, waits for them, and re-layouts  3.75 us (5%)
  other arithmetic  1.97 us (2%)
    pallas_call x1, Pallas kernels, on_device(): pl.pallas_call(functools.partial(exchange_kernel, heads, blocks, seq_coun...  54.9 us
    pallas_call x1, Pallas kernels, on_device(): pl.pallas_call(functools.partial(finish_kernel, heads, blocks, span), gri...  18 us

profile of v1, /device:TPU:29, one launch (start us, length us, event | category | flops | bytes accessed | tf_op | source)
XLA Modules:
  0.0 79.3 jit_solution(3460827617011662254)
XLA Ops:
  0.6 1.3 %dynamic_slice.3.doc_ref = s32[4]{0:T(128)} dynamic-slice(s32[32]{0:T(128)} %param.17, s32[]{:T(128)S(6)} %select_n.6), dynamic_slice_sizes={4} | dynamic-slice | bytes 36 | tf_op jit(solution)/shard_map/dynamic_slice | solution.py:415
  1.9 1.3 %maximum_bitcast_fusion.rate_ref = f32[1,64]{1,0:T(1,128)} fusion(f32[32]{0:T(128)} %param.11), kind=kLoop, calls=%fused_computation.2 | loop fusion | flops 64 | bytes 384 | tf_op jit(solution)/shard_map/reshape | solution.py:416
  3.2 0.7 compare_select_fusion
  3.9 1.1 %scatter_custom_fusion.order_ref = s32[8]{0:T(128)} fusion(s32[8]{0:T(128)S(1)} %compare_select_fusion, s32[8]{0:T(128)S(1)} %iota.3, s32[]{:T(128)} %constant.1.clone.1), kind=kCustom, calls=%fused_computation.3 | custom fusion | bytes 36 | tf_op jit(solution)/shard_map/scatter | solution.py:422
  5.0 0.7 broadcast_in_dim.7
  5.7 0.7 reshape_reshape.3.skip_ref
  6.4 54.9 %exchange.1 = (bf16[4,128,2048]{2,1,0:T(8,128)(2,1)}, bf16[4,128,2048]{2,1,0:T(8,128)(2,1)}, f32[8,2048]{1,0:T(8,128)}, bf16[1024,64]{1,0:T(8,128)(2,1)}, bf16[1...) custom-call(s32[4]{0:T(128)} %dynamic_slice.3.doc_ref, s32[8]{0:T(128)} %scatter_custom_fusion.order_ref, s32[8]{0:T(128)} %place_ref.1, ...), custom_call_target="tpu_custom_call" | custom-call | tf_op jit(solution)/shard_map/exchange/pallas_call | solution.py:430
  61.3 18.0 %finish.1 = (bf16[1024,2048]{1,0:T(8,128)(2,1)}, bf16[1024,2048]{1,0:T(8,128)(2,1)}, f32[1024,256]{1,0:T(8,128)}, f32[1024,256]{1,0:T(8,128)}) custom-call(s32[4]{0:T(128)} %dynamic_slice.3.doc_ref, bf16[1024,2048]{1,0:T(8,128)(2,1)} %x_ref.3, bf16[1024,2048]{1,0:T(8,128)(2,1)} %g_ref.3, bf16[1024,256]{1,0:T(8,128)(2,1)} %b_ref.3, bf16[1024,256]{1,0:T(8,128)(2,1)} %c_ref.3, ...), custom_call_target="tpu_custom_call" | custom-call | tf_op jit(solution)/shard_map/finish/pallas_call | solution.py:536
  (1 shorter events, 0.0 us)

commit v2 on v1

v2 whole, which is shorter than its diff:
```python
import functools

import jax
import jax.numpy as jnp
from jax import lax
from jax.experimental import pallas as pl
from jax.experimental.pallas import tpu as pltpu
from jax.sharding import PartitionSpec as P

HEADS = 128
HEAD_DIM = 64
STATE = 128
GROUPS = 8
BLOCK = 256
CHUNK = 256
EXTRA = 16
VMEM_LIMIT = 60 * 1024 * 1024

F32 = jnp.float32
BF16 = jnp.bfloat16


def partner(block, axis, bit):
    count = lax.axis_size(axis)
    route = []
    for low in range(count):
        high = low | 1 << bit
        if high != low and high < count:
            route += [(low, high), (high, low)]
    return lax.ppermute(block, axis, route)


def dot_nn(a, b):
    return lax.dot_general(a, b, (((1,), (0,)), ((), ())), preferred_element_type=F32)


def dot_nt(a, b):
    return lax.dot_general(a, b, (((1,), (1,)), ((), ())), preferred_element_type=F32)


def dot_tn(a, b):
    return lax.dot_general(a, b, (((0,), (0,)), ((), ())), preferred_element_type=F32)


def iota(shape, dim):
    return lax.broadcasted_iota(jnp.int32, shape, dim)


def head_spread(heads, first_head, width):
    row = iota((heads, width), 0)
    return (row == first_head + iota((heads, width), 1) // HEAD_DIM).astype(F32).astype(BF16)


def head_spread_halves(heads, first_head, width):
    row = iota((2 * heads, width), 0)
    row = jnp.where(row >= heads, row - heads, row)
    return (row == first_head + iota((2 * heads, width), 1) // HEAD_DIM).astype(F32).astype(BF16)


def three_parts(value):
    high = value.astype(BF16)
    rest = value - high.astype(F32)
    mid = rest.astype(BF16)
    return high, mid, (rest - mid.astype(F32)).astype(BF16)


def spread_row(row, matrix):
    tall = jnp.broadcast_to(row, (8, row.shape[1]))
    return sum(dot_nn(part, matrix) for part in three_parts(tall))[0:1, :]


def token_setup(blocks, base, doc_ref, step_ref, rate_ref, e_ref, f_ref, whole_e_ref, whole_f_ref):
    heads = step_ref.shape[0]
    row, col = iota((heads, 2 * heads), 0), iota((heads, 2 * heads), 1)
    twice = ((row == col) | (row + heads == col)).astype(F32).astype(BF16)
    rate = spread_row(rate_ref[...], twice)
    row, col = iota((BLOCK, BLOCK), 0), iota((BLOCK, BLOCK), 1)
    lower = (row >= col).astype(F32).astype(BF16)
    eye = (row == col).astype(F32).astype(BF16)
    left = iota((BLOCK, 2 * heads), 1) < heads
    position = iota((BLOCK, 2 * heads), 0)

    def halves(value):
        top = value.astype(BF16).astype(F32)
        return jnp.where(left, top, value - top).astype(BF16)

    lead = jnp.ones((1, 2 * heads), F32)
    weights = []
    for k in range(blocks):
        rows = pl.ds(k * BLOCK, BLOCK)
        doc = doc_ref[base + k]
        step = step_ref[:, rows]
        parts = three_parts(jnp.concatenate([step, step], axis=0))
        cum = -rate * sum(dot_nt(lower, part) for part in parts)
        e = jnp.exp(cum)
        f = sum(dot_nt(eye, part) for part in parts) * jnp.exp(-cum)
        last = e[BLOCK - 1 : BLOCK, :]
        decay = jnp.where(doc == BLOCK, last, 0.0)
        e_ref[rows, :] = halves(e)
        f_ref[rows, :] = halves(f)
        whole_e_ref[rows, :] = halves(lead * jnp.where(position < doc, e, 0.0))
        lead = lead * decay
        weights.append((jnp.where(position >= doc, last * f, 0.0), decay))
    tail = jnp.ones((1, 2 * heads), F32)
    for k in reversed(range(blocks)):
        whole_f_ref[pl.ds(k * BLOCK, BLOCK), :] = halves(tail * weights[k][0])
        tail = tail * weights[k][1]


def summary(
    blocks, base, chunk, slot, lanes, doc_ref, x_ref, g_ref, b_ref, c_ref, e_ref, f_ref, msg_ref, pre_ref, suf_ref
):
    spread = head_spread_halves(e_ref.shape[1] // 2, chunk * (CHUNK // HEAD_DIM), CHUNK)
    position = iota((BLOCK, STATE), 0)
    ends, reads, decays, lasts = [], [], [], []
    for k in range(blocks):
        rows = pl.ds(k * BLOCK, BLOCK)
        doc = doc_ref[base + k]
        e_wide = dot_nn(e_ref[rows, :], spread)
        f_wide = dot_nn(f_ref[rows, :], spread)
        grad_in = (e_wide * g_ref[rows, :].astype(F32)).astype(BF16)
        data_in = (f_wide * x_ref[rows, :].astype(F32)).astype(BF16)
        write = jnp.where(position >= doc, b_ref[rows, :].astype(F32), 0.0).astype(BF16)
        read = jnp.where(position < doc, c_ref[rows, :].astype(F32), 0.0).astype(BF16)
        last = e_wide[BLOCK - 1 : BLOCK, :]
        ends.append(last * dot_tn(write, data_in))
        reads.append(dot_tn(read, grad_in))
        decays.append(jnp.where(doc == BLOCK, last, 0.0))
        lasts.append(last)
    state = jnp.zeros((STATE, CHUNK), F32)
    lead = jnp.ones((1, CHUNK), F32)
    for k in range(blocks):
        pre_ref[k, :, lanes] = state.astype(BF16)
        state = decays[k] * state + ends[k]
        lead = lead * decays[k]
    grad = jnp.zeros((STATE, CHUNK), F32)
    for k in reversed(range(blocks)):
        suf_ref[k, :, lanes] = (lasts[k] * grad).astype(BF16)
        grad = reads[k] + decays[k] * grad
    msg_ref[slot, :STATE, :] = state.astype(BF16)
    msg_ref[slot, STATE : 2 * STATE, :] = grad.astype(BF16)
    full = jnp.broadcast_to(lead, (EXTRA, CHUNK))
    top = full.astype(BF16).astype(F32)
    msg_ref[slot, 2 * STATE :, :] = jnp.where(iota((EXTRA, CHUNK), 0) == 0, top, full - top).astype(BF16)


def inner_block(
    doc, first_head, e, f, x_ref, g_ref, b_ref, c_ref, state, grad, skip_ref, y_ref, dx_ref, dw_ref, dr_ref
):
    heads = e.shape[1] // 2
    width = x_ref.shape[1]
    spread = head_spread_halves(heads, first_head, width)
    e_wide, f_wide = dot_nn(e, spread), dot_nn(f, spread)
    skip = spread_row(skip_ref[...], head_spread(heads, first_head, width))
    x, g = x_ref[...].astype(F32), g_ref[...].astype(F32)
    grad_in = (e_wide * g).astype(BF16)
    data_in = (f_wide * x).astype(BF16)
    position = iota((BLOCK, STATE), 0)
    b, c = b_ref[...], c_ref[...]
    write_on, read_on = position >= doc, position < doc
    write = jnp.where(write_on, b.astype(F32), 0.0).astype(BF16)
    read = jnp.where(read_on, c.astype(F32), 0.0).astype(BF16)
    row, col = iota((BLOCK, BLOCK), 0), iota((BLOCK, BLOCK), 1)
    keep = (row >= col) & ((row < doc) | (col >= doc))
    keep_t = (col >= row) & ((col < doc) | (row >= doc))
    score = jnp.where(keep, dot_nt(c, b), 0.0).astype(BF16)
    score_t = jnp.where(keep_t, dot_nt(b, c), 0.0).astype(BF16)
    y_ref[...] = (e_wide * (dot_nn(score, data_in) + dot_nn(read, state)) + skip * x).astype(BF16)
    dx_ref[...] = (f_wide * (dot_nn(score_t, grad_in) + dot_nn(write, grad)) + skip * g).astype(BF16)
    score_grad = jnp.where(keep, dot_nt(grad_in, data_in), 0.0).astype(BF16)
    dw_ref[...] = dot_tn(score_grad, c) + jnp.where(write_on, dot_nt(data_in, grad), 0.0)
    dr_ref[...] = dot_nn(score_grad, b) + jnp.where(read_on, dot_nt(grad_in, state), 0.0)


def summary_kernel(
    blocks, doc_ref, x_ref, g_ref, b_ref, c_ref, step_ref, rate_ref, msg_ref, pre_ref, suf_ref, e_ref, f_ref, we_ref, wf_ref
):
    chunk = pl.program_id(0)
    base = lax.axis_index("seq") * blocks

    @pl.when(chunk == 0)
    def _():
        token_setup(blocks, base, doc_ref, step_ref, rate_ref, e_ref, f_ref, we_ref, wf_ref)

    lanes = slice(None)
    summary(blocks, base, chunk, 0, lanes, doc_ref, x_ref, g_ref, b_ref, c_ref, e_ref, f_ref, msg_ref, pre_ref, suf_ref)


def inner_kernel(
    blocks, span, doc_ref, x_ref, g_ref, b_ref, c_ref, e_ref, f_ref, pre_ref, suf_ref, skip_ref, y_ref, dx_ref, dw_ref, dr_ref
):
    group, k = pl.program_id(0), pl.program_id(1)
    doc = doc_ref[lax.axis_index("seq") * blocks + k]
    inner_block(
        doc, group * span, e_ref[...], f_ref[...], x_ref, g_ref, b_ref, c_ref, pre_ref[0], suf_ref[0], skip_ref, y_ref, dx_ref, dw_ref, dr_ref
    )


def shard_at(place_ref, count, place):
    found = 0
    for shard in range(1, count):
        found = jnp.where(place_ref[shard] == place, shard, found)
    return found


def chain_kernel(count, order_ref, got_ref, out_ref):
    width = got_ref.shape[-1]

    def decay_of(shard):
        pair = got_ref[shard, 2 * STATE :, :].astype(F32)
        return pair[0:1, :] + pair[1:2, :]

    def forward(place, state):
        shard = order_ref[place]
        out_ref[shard, :STATE, :] = state.astype(BF16)
        return decay_of(shard) * state + got_ref[shard, :STATE, :].astype(F32)

    def backward(step, grad):
        shard = order_ref[count - 1 - step]
        out_ref[shard, STATE:, :] = grad.astype(BF16)
        return decay_of(shard) * grad + got_ref[shard, STATE : 2 * STATE, :].astype(F32)

    empty = jnp.zeros((STATE, width), F32)
    lax.fori_loop(0, count, forward, empty)
    lax.fori_loop(0, count, backward, empty)


def owner_at(step, count):
    return lax.rem(step, 2) * (count // 2) + step // 2


def exchange_kernel(
    blocks,
    span,
    groups,
    count,
    doc_ref,
    place_ref,
    x_ref,
    g_ref,
    b_ref,
    c_ref,
    step_ref,
    rate_ref,
    skip_ref,
    bx_ref,
    bg_ref,
    bb_ref,
    bc_ref,
    we_ref,
    wf_ref,
    dev_ref,
    y_ref,
    dx_ref,
    dw_ref,
    dr_ref,
    e_ref,
    f_ref,
    pre,
    suf,
    msg,
    got,
    chain,
    answer,
    back,
    send_sem,
    recv_sem,
    back_send_sem,
    back_recv_sem,
):
    step = pl.program_id(0)
    me = lax.axis_index("seq")
    base = me * blocks
    barrier = pltpu.get_barrier_semaphore()
    steps = count + groups * blocks

    def outward(owner, source):
        return pltpu.make_async_remote_copy(
            src_ref=msg.at[owner],
            dst_ref=got.at[source],
            send_sem=send_sem.at[owner],
            recv_sem=recv_sem.at[source],
            device_id={"seq": owner},
            device_id_type=pl.DeviceIdType.MESH,
        )

    def homeward(shard, source):
        return pltpu.make_async_remote_copy(
            src_ref=answer.at[shard],
            dst_ref=back.at[source],
            send_sem=back_send_sem.at[shard],
            recv_sem=back_recv_sem.at[source],
            device_id={"seq": shard},
            device_id_type=pl.DeviceIdType.MESH,
        )

    @pl.when(step == 0)
    def _():
        for ahead in range(1, count):
            pl.semaphore_signal(
                barrier,
                inc=1,
                device_id={"seq": lax.rem(me + ahead, count)},
                device_id_type=pl.DeviceIdType.MESH,
            )
        token_setup(blocks, base, doc_ref, step_ref, rate_ref, e_ref, f_ref, we_ref, wf_ref)

    @pl.when(step < count)
    def _():
        owner = owner_at(step, count)
        lanes = pl.ds(pl.multiple_of(owner * CHUNK, CHUNK), CHUNK)
        summary(
            blocks, base, owner, owner, lanes, doc_ref, x_ref, g_ref, b_ref, c_ref, e_ref, f_ref, msg, pre, suf
        )

        @pl.when(step == 0)
        def _():
            pl.semaphore_wait(barrier, count - 1)

        @pl.when(owner != me)
        def _():
            outward(owner, me).start()

        @pl.when(owner == me)
        def _():
            got[me] = msg[owner]

    @pl.when((step >= count) & (step < steps))
    def _():
        group = (step - count) // blocks
        k = lax.rem(step - count, blocks)
        rows = pl.ds(pl.multiple_of(k * BLOCK, BLOCK), BLOCK)
        wide = span * HEAD_DIM
        lanes = pl.ds(pl.multiple_of(group * wide, wide), wide)
        inner_block(
            doc_ref[base + k],
            group * span,
            e_ref[rows, :],
            f_ref[rows, :],
            bx_ref,
            bg_ref,
            bb_ref,
            bc_ref,
            pre[k, :, lanes],
            suf[k, :, lanes],
            skip_ref,
            y_ref,
            dx_ref,
            dw_ref,
            dr_ref,
        )

    half = count // 2
    turn = 2 * lax.rem(me, half) + me // half
    early = half + 1
    chain_step = early + (turn * (steps - 1 - early)) // (count - 1)

    @pl.when(step == chain_step)
    def _():
        for shard in range(count):

            @pl.when(me != shard)
            def _():
                outward(shard, shard).wait_recv()

        def decay_of(shard):
            pair = got[shard, 2 * STATE :, :].astype(F32)
            return pair[0:1, :] + pair[1:2, :]

        order = [shard_at(place_ref, count, place) for place in range(count)]
        state = jnp.zeros((STATE, CHUNK), F32)
        for place in range(count):
            shard = order[place]
            chain[place, :STATE, :] = state.astype(BF16)
            state = decay_of(shard) * state + got[shard, :STATE, :].astype(F32)
        grad = jnp.zeros((STATE, CHUNK), F32)
        for place in reversed(range(count)):
            shard = order[place]
            chain[place, STATE:, :] = grad.astype(BF16)
            grad = decay_of(shard) * grad + got[shard, STATE : 2 * STATE, :].astype(F32)
        for shard in range(count):
            answer[shard] = chain[place_ref[shard]]

            @pl.when(me != shard)
            def _():
                homeward(shard, me).start()

        back[me] = answer[me]

    @pl.when(step == steps)
    def _():
        for shard in range(count):

            @pl.when(me != shard)
            def _():
                homeward(shard, shard).wait_recv()

        for shard in range(count):

            @pl.when(me != shard)
            def _():
                outward(shard, me).wait_send()
                homeward(shard, me).wait_send()

        dev_ref[...] = back[...]


def finish_kernel(
    span, x_ref, g_ref, b_ref, c_ref, e_ref, f_ref, dev_ref, yp_ref, dxp_ref, dwp_ref, drp_ref, y_ref, dx_ref, dw_ref, dr_ref
):
    spread = head_spread_halves(e_ref.shape[1] // 2, pl.program_id(0) * span, span * HEAD_DIM)
    e_wide = dot_nn(e_ref[...], spread)
    f_wide = dot_nn(f_ref[...], spread)
    grad_in = (e_wide * g_ref[...].astype(F32)).astype(BF16)
    data_in = (f_wide * x_ref[...].astype(F32)).astype(BF16)
    parts = range(dev_ref.shape[0])
    state = jnp.concatenate([dev_ref[j, :STATE, :] for j in parts], axis=1)
    grad = jnp.concatenate([dev_ref[j, STATE:, :] for j in parts], axis=1)
    y_ref[...] = (yp_ref[...].astype(F32) + e_wide * dot_nn(c_ref[...], state)).astype(BF16)
    dx_ref[...] = (dxp_ref[...].astype(F32) + f_wide * dot_nn(b_ref[...], grad)).astype(BF16)
    dw_ref[...] = dwp_ref[...] + dot_nt(data_in, grad)
    dr_ref[...] = drp_ref[...] + dot_nt(grad_in, state)


def on_device(
    seq_input,
    step_size,
    decay_rate,
    skip_gain,
    state_write,
    state_read,
    out_grad,
    segment_order,
    doc_start,
):
    heads = decay_rate.shape[0]
    group_heads = HEADS // GROUPS
    span = min(heads, group_heads)
    groups = heads // span
    group_devices = max(1, group_heads // heads)
    levels = group_devices.bit_length() - 1
    tokens = seq_input.shape[0]
    blocks = tokens // BLOCK
    channels = heads * HEAD_DIM
    chunks = channels // CHUNK
    group_chunks = chunks // groups
    seq_count = lax.axis_size("seq")
    head_rank = lax.axis_index("head")
    own_write, own_read = (state_write, state_read)
    for level in range(levels):
        other_write, other_read = partner((own_write, own_read), "head", level)
        upper_half = head_rank >> level & 1 == 1
        own_write = jnp.where(
            upper_half,
            jnp.concatenate([other_write, own_write], 1),
            jnp.concatenate([own_write, other_write], 1),
        )
        own_read = jnp.where(
            upper_half,
            jnp.concatenate([other_read, own_read], 1),
            jnp.concatenate([own_read, other_read], 1),
        )
    rate_row = decay_rate.reshape(1, heads)
    skip_row = skip_gain.reshape(1, heads)
    smem = pl.BlockSpec(memory_space=pltpu.SMEM)
    params = pltpu.CompilerParams(vmem_limit_bytes=VMEM_LIMIT)
    rows = 2 * STATE + EXTRA
    lanes = span * HEAD_DIM
    column_shape = jax.ShapeDtypeStruct((tokens, 2 * heads), BF16)
    part_shapes = (
        jax.ShapeDtypeStruct((tokens, channels), BF16),
        jax.ShapeDtypeStruct((tokens, channels), BF16),
        jax.ShapeDtypeStruct((tokens, groups * STATE), F32),
        jax.ShapeDtypeStruct((tokens, groups * STATE), F32),
    )

    def whole_spec(shape):
        return pl.BlockSpec(shape, lambda *place: (0,) * len(shape))

    def part_specs(where):
        return (
            pl.BlockSpec((BLOCK, lanes), where),
            pl.BlockSpec((BLOCK, lanes), where),
            pl.BlockSpec((BLOCK, STATE), where),
            pl.BlockSpec((BLOCK, STATE), where),
        )

    def chunk_specs(chunk_of):
        return [
            pl.BlockSpec((tokens, CHUNK), lambda i: (0, chunk_of(i))),
            pl.BlockSpec((tokens, CHUNK), lambda i: (0, chunk_of(i))),
            pl.BlockSpec((tokens, STATE), lambda i: (0, chunk_of(i) // group_chunks)),
            pl.BlockSpec((tokens, STATE), lambda i: (0, chunk_of(i) // group_chunks)),
        ]

    def by_block(g, k):
        return (k, g)

    tables = [whole_spec((heads, tokens)), whole_spec((1, heads))]
    if chunks == seq_count:

        def served(i):
            return owner_at(jnp.minimum(i, chunks - 1), chunks)

        def block_of(i):
            place = jnp.clip(i - chunks, 0, groups * blocks - 1)
            return (lax.rem(place, blocks), place // blocks)

        whole_e, whole_f, device, *parts = pl.pallas_call(
            functools.partial(exchange_kernel, blocks, span, groups, seq_count),
            grid=(chunks + groups * blocks + 1,),
            out_shape=(
                column_shape,
                column_shape,
                jax.ShapeDtypeStruct((chunks, 2 * STATE, CHUNK), BF16),
                *part_shapes,
            ),
            in_specs=[smem, smem, *chunk_specs(served), *tables, whole_spec((1, heads)), *part_specs(block_of)],
            out_specs=(
                whole_spec((tokens, 2 * heads)),
                whole_spec((tokens, 2 * heads)),
                whole_spec((chunks, 2 * STATE, CHUNK)),
                *part_specs(block_of),
            ),
            scratch_shapes=[
                pltpu.VMEM((tokens, 2 * heads), BF16),
                pltpu.VMEM((tokens, 2 * heads), BF16),
                pltpu.VMEM((blocks, STATE, channels), BF16),
                pltpu.VMEM((blocks, STATE, channels), BF16),
                pltpu.VMEM((chunks, rows, CHUNK), BF16),
                pltpu.VMEM((chunks, rows, CHUNK), BF16),
                pltpu.VMEM((chunks, 2 * STATE, CHUNK), BF16),
                pltpu.VMEM((chunks, 2 * STATE, CHUNK), BF16),
                pltpu.VMEM((chunks, 2 * STATE, CHUNK), BF16),
                pltpu.SemaphoreType.DMA((chunks,)),
                pltpu.SemaphoreType.DMA((chunks,)),
                pltpu.SemaphoreType.DMA((chunks,)),
                pltpu.SemaphoreType.DMA((chunks,)),
            ],
            compiler_params=pltpu.CompilerParams(
                vmem_limit_bytes=VMEM_LIMIT, collective_id=0, has_side_effects=True
            ),
            name="exchange",
        )(
            doc_start,
            segment_order,
            seq_input,
            out_grad,
            own_write,
            own_read,
            step_size,
            rate_row,
            skip_row,
            seq_input,
            out_grad,
            own_write,
            own_read,
        )
    else:
        state_shape = jax.ShapeDtypeStruct((blocks, STATE, channels), BF16)
        message, pre, suf, e_cols, f_cols, whole_e, whole_f = pl.pallas_call(
            functools.partial(summary_kernel, blocks),
            grid=(chunks,),
            out_shape=(
                jax.ShapeDtypeStruct((chunks, rows, CHUNK), BF16),
                state_shape,
                state_shape,
                *[column_shape] * 4,
            ),
            in_specs=[smem, *chunk_specs(lambda i: i), *tables],
            out_specs=(
                pl.BlockSpec((1, rows, CHUNK), lambda i: (i, 0, 0)),
                pl.BlockSpec((blocks, STATE, CHUNK), lambda i: (0, 0, i)),
                pl.BlockSpec((blocks, STATE, CHUNK), lambda i: (0, 0, i)),
                *[whole_spec((tokens, 2 * heads))] * 4,
            ),
            compiler_params=params,
            name="summary",
        )(doc_start, seq_input, out_grad, own_write, own_read, step_size, rate_row)
        width = channels // seq_count
        message = jnp.transpose(message, (1, 0, 2)).reshape(rows, seq_count, width)
        message = jnp.transpose(message, (1, 0, 2))
        got = lax.all_to_all(message, "seq", split_axis=0, concat_axis=0, tiled=True)
        parts = pl.pallas_call(
            functools.partial(inner_kernel, blocks, span),
            grid=(groups, blocks),
            out_shape=part_shapes,
            in_specs=[
                smem,
                *part_specs(by_block),
                pl.BlockSpec((BLOCK, 2 * heads), lambda g, k: (k, 0)),
                pl.BlockSpec((BLOCK, 2 * heads), lambda g, k: (k, 0)),
                pl.BlockSpec((1, STATE, lanes), lambda g, k: (k, 0, g)),
                pl.BlockSpec((1, STATE, lanes), lambda g, k: (k, 0, g)),
                whole_spec((1, heads)),
            ],
            out_specs=part_specs(by_block),
            compiler_params=params,
            name="inner",
        )(doc_start, seq_input, out_grad, own_write, own_read, e_cols, f_cols, pre, suf, skip_row)
        order = jnp.zeros((seq_count,), jnp.int32).at[segment_order].set(
            jnp.arange(seq_count, dtype=jnp.int32)
        )
        answer = pl.pallas_call(
            functools.partial(chain_kernel, seq_count),
            out_shape=jax.ShapeDtypeStruct((seq_count, 2 * STATE, width), BF16),
            in_specs=[smem, pl.BlockSpec(memory_space=pltpu.VMEM)],
            out_specs=pl.BlockSpec(memory_space=pltpu.VMEM),
            compiler_params=params,
            name="chain",
        )(order, got)
        device = lax.all_to_all(answer, "seq", split_axis=0, concat_axis=0, tiled=True)
        device = jnp.transpose(device, (1, 0, 2)).reshape(2 * STATE, chunks, CHUNK)
        device = jnp.transpose(device, (1, 0, 2))

    mixed, input_grad, write_sum, read_sum = pl.pallas_call(
        functools.partial(finish_kernel, span),
        grid=(groups, blocks),
        out_shape=part_shapes,
        in_specs=[
            *part_specs(by_block),
            pl.BlockSpec((BLOCK, 2 * heads), lambda g, k: (k, 0)),
            pl.BlockSpec((BLOCK, 2 * heads), lambda g, k: (k, 0)),
            pl.BlockSpec((group_chunks, 2 * STATE, CHUNK), lambda g, k: (g, 0, 0)),
            *part_specs(by_block),
        ],
        out_specs=part_specs(by_block),
        compiler_params=params,
        name="finish",
    )(seq_input, out_grad, own_write, own_read, whole_e, whole_f, device, *parts)

    for level in range(levels):
        other_write_sum, other_read_sum = partner(
            (write_sum.astype(BF16), read_sum.astype(BF16)), "head", level
        )
        write_sum = write_sum + other_write_sum.astype(F32)
        read_sum = read_sum + other_read_sum.astype(F32)
    own_width = groups * STATE // group_devices
    if group_devices > 1:
        own_first = head_rank % group_devices * own_width
        write_sum = lax.dynamic_slice_in_dim(write_sum, own_first, own_width, 1)
        read_sum = lax.dynamic_slice_in_dim(read_sum, own_first, own_width, 1)
    return mixed, input_grad, write_sum, read_sum


def solution(mesh):
    placed = (
        P("seq", "head"),
        P("head", "seq"),
        P("head"),
        P("head"),
        P("seq", "head"),
        P("seq", "head"),
        P("seq", "head"),
        P(),
        P(),
    )
    return jax.shard_map(
        on_device,
        mesh=mesh,
        in_specs=placed,
        out_specs=(P("seq", "head"), P("seq", "head"), P("seq", "head"), P("seq", "head")),
        check_vma=False,
    )
```

time: 79.7 us -> 73.4 us (0.921)
  the two profiles are of different devices: /device:TPU:29 before, /device:TPU:17 now
where the time goes in v2:
time: 73.4 us; the launch traced here: 73.1 us
  Pallas kernels  72.5 us (99%)
    pallas_call x1, Pallas kernels, on_device(): pl.pallas_call(functools.partial(exchange_kernel, blocks, span, groups, s...  57.7 us
    pallas_call x1, Pallas kernels, on_device(): pl.pallas_call(functools.partial(finish_kernel, span), grid=(groups, bloc...  14.8 us

profile of v2, /device:TPU:17, one launch (start us, length us, event | category | flops | bytes accessed | tf_op | source)
XLA Modules:
  0.0 73.1 jit_solution(6796645122661523365)
XLA Ops:
  0.6 57.7 %exchange.1 = (bf16[1024,64]{1,0:T(8,128)(2,1)}, bf16[1024,64]{1,0:T(8,128)(2,1)}, bf16[8,256,256]{2,1,0:T(8,128)(2,1)}, bf16[1024,2048]{1,0:T(8,128)(2,1)}, bf1...) custom-call(s32[32]{0:T(128)} %doc_ref.1, s32[8]{0:T(128)} %place_ref.1, ...), custom_call_target="tpu_custom_call" | custom-call | tf_op jit(solution)/shard_map/exchange/pallas_call | solution.py:509
  58.3 14.8 %finish.1 = (bf16[1024,2048]{1,0:T(8,128)(2,1)}, bf16[1024,2048]{1,0:T(8,128)(2,1)}, f32[1024,256]{1,0:T(8,128)}, f32[1024,256]{1,0:T(8,128)}) custom-call(bf16[1024,2048]{1,0:T(8,128)(2,1)} %x_ref.3, bf16[1024,2048]{1,0:T(8,128)(2,1)} %g_ref.3, bf16[1024,256]{1,0:T(8,128)(2,1)} %b_ref.3, bf16[1024,256]{1,0:T(8,128)(2,1)} %c_ref.3, ...), custom_call_target="tpu_custom_call" | custom-call | tf_op jit(solution)/shard_map/finish/pallas_call | solution.py:616

commit v3 on v2

--- a/solution.py
+++ b/solution.py
@@ -108,7 +108,7 @@
 
 
 def summary(
-    blocks, base, chunk, slot, lanes, doc_ref, x_ref, g_ref, b_ref, c_ref, e_ref, f_ref, msg_ref, pre_ref, suf_ref
+    blocks, base, chunk, slot, lanes, doc_ref, x_ref, g_ref, b_ref, c_ref, e_ref, f_ref, msg_ref, pre_ref, suf_ref, scale_ref
 ):
     spread = head_spread_halves(e_ref.shape[1] // 2, chunk * (CHUNK // HEAD_DIM), CHUNK)
     position = iota((BLOCK, STATE), 0)
@@ -131,12 +131,16 @@
     lead = jnp.ones((1, CHUNK), F32)
     for k in range(blocks):
         pre_ref[k, :, lanes] = state.astype(BF16)
+        scale_ref[k, 0:8, lanes] = jnp.broadcast_to(lead, (8, CHUNK))
         state = decays[k] * state + ends[k]
         lead = lead * decays[k]
     grad = jnp.zeros((STATE, CHUNK), F32)
+    tail = jnp.ones((1, CHUNK), F32)
     for k in reversed(range(blocks)):
         suf_ref[k, :, lanes] = (lasts[k] * grad).astype(BF16)
+        scale_ref[k, 8:16, lanes] = jnp.broadcast_to(lasts[k] * tail, (8, CHUNK))
         grad = reads[k] + decays[k] * grad
+        tail = tail * decays[k]
     msg_ref[slot, :STATE, :] = state.astype(BF16)
     msg_ref[slot, STATE : 2 * STATE, :] = grad.astype(BF16)
     full = jnp.broadcast_to(lead, (EXTRA, CHUNK))
@@ -173,7 +177,7 @@
 
 
 def summary_kernel(
-    blocks, doc_ref, x_ref, g_ref, b_ref, c_ref, step_ref, rate_ref, msg_ref, pre_ref, suf_ref, e_ref, f_ref, we_ref, wf_ref
+    blocks, doc_ref, x_ref, g_ref, b_ref, c_ref, step_ref, rate_ref, msg_ref, pre_ref, suf_ref, e_ref, f_ref, we_ref, wf_ref, scale
 ):
     chunk = pl.program_id(0)
     base = lax.axis_index("seq") * blocks
@@ -183,7 +187,7 @@
         token_setup(blocks, base, doc_ref, step_ref, rate_ref, e_ref, f_ref, we_ref, wf_ref)
 
     lanes = slice(None)
-    summary(blocks, base, chunk, 0, lanes, doc_ref, x_ref, g_ref, b_ref, c_ref, e_ref, f_ref, msg_ref, pre_ref, suf_ref)
+    summary(blocks, base, chunk, 0, lanes, doc_ref, x_ref, g_ref, b_ref, c_ref, e_ref, f_ref, msg_ref, pre_ref, suf_ref, scale)
 
 
 def inner_kernel(
@@ -225,8 +229,9 @@
     lax.fori_loop(0, count, backward, empty)
 
 
-def owner_at(step, count):
-    return lax.rem(step, 2) * (count // 2) + step // 2
+def owner_of(chunk, groups, count):
+    each = count // groups
+    return lax.rem(chunk, each) * groups + chunk // each
 
 
 def exchange_kernel(
@@ -258,6 +263,7 @@
     f_ref,
     pre,
     suf,
+    scale,
     msg,
     got,
     chain,
@@ -274,25 +280,28 @@
     barrier = pltpu.get_barrier_semaphore()
     steps = count + groups * blocks
 
-    def outward(owner, source):
+    def outward(chunk, source):
         return pltpu.make_async_remote_copy(
-            src_ref=msg.at[owner],
+            src_ref=msg.at[chunk],
             dst_ref=got.at[source],
-            send_sem=send_sem.at[owner],
+            send_sem=send_sem.at[chunk],
             recv_sem=recv_sem.at[source],
-            device_id={"seq": owner},
+            device_id={"seq": owner_of(chunk, groups, count)},
             device_id_type=pl.DeviceIdType.MESH,
         )
 
-    def homeward(shard, source):
+    def homeward(shard, chunk):
         return pltpu.make_async_remote_copy(
             src_ref=answer.at[shard],
-            dst_ref=back.at[source],
+            dst_ref=back.at[chunk],
             send_sem=back_send_sem.at[shard],
-            recv_sem=back_recv_sem.at[source],
+            recv_sem=back_recv_sem.at[chunk],
             device_id={"seq": shard},
             device_id_type=pl.DeviceIdType.MESH,
         )
+
+    each = count // groups
+    mine = lax.rem(me, groups) * each + me // groups
 
     @pl.when(step == 0)
     def _():
@@ -307,53 +316,27 @@
 
     @pl.when(step < count)
     def _():
-        owner = owner_at(step, count)
-        lanes = pl.ds(pl.multiple_of(owner * CHUNK, CHUNK), CHUNK)
+        lanes = pl.ds(pl.multiple_of(step * CHUNK, CHUNK), CHUNK)
         summary(
-            blocks, base, owner, owner, lanes, doc_ref, x_ref, g_ref, b_ref, c_ref, e_ref, f_ref, msg, pre, suf
+            blocks, base, step, step, lanes, doc_ref, x_ref, g_ref, b_ref, c_ref, e_ref, f_ref, msg, pre, suf, scale
         )
 
         @pl.when(step == 0)
         def _():
             pl.semaphore_wait(barrier, count - 1)
 
-        @pl.when(owner != me)
+        @pl.when(step != mine)
         def _():
-            outward(owner, me).start()
-
-        @pl.when(owner == me)
+            outward(step, me).start()
+
+        @pl.when(step == mine)
         def _():
-            got[me] = msg[owner]
-
-    @pl.when((step >= count) & (step < steps))
-    def _():
-        group = (step - count) // blocks
-        k = lax.rem(step - count, blocks)
-        rows = pl.ds(pl.multiple_of(k * BLOCK, BLOCK), BLOCK)
-        wide = span * HEAD_DIM
-        lanes = pl.ds(pl.multiple_of(group * wide, wide), wide)
-        inner_block(
-            doc_ref[base + k],
-            group * span,
-            e_ref[rows, :],
-            f_ref[rows, :],
-            bx_ref,
-            bg_ref,
-            bb_ref,
-            bc_ref,
-            pre[k, :, lanes],
-            suf[k, :, lanes],
-            skip_ref,
-            y_ref,
-            dx_ref,
-            dw_ref,
-            dr_ref,
-        )
-
-    half = count // 2
-    turn = 2 * lax.rem(me, half) + me // half
-    early = half + 1
-    chain_step = early + (turn * (steps - 1 - early)) // (count - 1)
+            got[me] = msg[step]
+
+    full_step = count + blocks
+    chain_step = jnp.where(
+        mine >= count - each, full_step, jnp.minimum(count // 2 + 1 + mine, full_step)
+    )
 
     @pl.when(step == chain_step)
     def _():
@@ -361,7 +344,7 @@
 
             @pl.when(me != shard)
             def _():
-                outward(shard, shard).wait_recv()
+                outward((shard % groups) * each + shard // groups, shard).wait_recv()
 
         def decay_of(shard):
             pair = got[shard, 2 * STATE :, :].astype(F32)
@@ -383,43 +366,110 @@
 
             @pl.when(me != shard)
             def _():
-                homeward(shard, me).start()
-
-        back[me] = answer[me]
+                homeward(shard, mine).start()
+
+        back[mine] = answer[me]
+
+    def wait_back(first, last):
+        for chunk in range(first, last):
+
+            @pl.when(mine != chunk)
+            def _():
+                homeward((chunk % each) * groups + chunk // each, chunk).wait_recv()
+
+    wide = span * HEAD_DIM
+
+    def run_block(state, grad, group, k, rows):
+        inner_block(
+            doc_ref[base + k],
+            group * span,
+            e_ref[rows, :],
+            f_ref[rows, :],
+            bx_ref,
+            bg_ref,
+            bb_ref,
+            bc_ref,
+            state,
+            grad,
+            skip_ref,
+            y_ref,
+            dx_ref,
+            dw_ref,
+            dr_ref,
+        )
+
+    @pl.when((step >= count) & (step < full_step))
+    def _():
+        k = step - count
+        rows = pl.ds(pl.multiple_of(k * BLOCK, BLOCK), BLOCK)
+        lanes = pl.ds((groups - 1) * wide, wide)
+        run_block(pre[k, :, lanes], suf[k, :, lanes], groups - 1, k, rows)
+
+    if groups > 1:
+
+        @pl.when(step == full_step)
+        def _():
+            wait_back(0, count - each)
+
+        @pl.when((step >= full_step) & (step < steps))
+        def _():
+            group = (step - full_step) // blocks
+            k = lax.rem(step - full_step, blocks)
+            rows = pl.ds(pl.multiple_of(k * BLOCK, BLOCK), BLOCK)
+            lanes = pl.ds(pl.multiple_of(group * wide, wide), wide)
+            chunks = [back[group * each + j] for j in range(each)]
+            state_in = jnp.concatenate([part[:STATE] for part in chunks], axis=1)
+            grad_in = jnp.concatenate([part[STATE:] for part in chunks], axis=1)
+            lead, tail = scale[k, 0:1, lanes], scale[k, 8:9, lanes]
+            state = pre[k, :, lanes].astype(F32) + lead * state_in.astype(F32)
+            grad = suf[k, :, lanes].astype(F32) + tail * grad_in.astype(F32)
+            run_block(state.astype(BF16), grad.astype(BF16), group, k, rows)
 
     @pl.when(step == steps)
     def _():
+        wait_back(count - each, count)
+        for chunk in range(count):
+
+            @pl.when(mine != chunk)
+            def _():
+                outward(chunk, me).wait_send()
+
         for shard in range(count):
 
             @pl.when(me != shard)
             def _():
-                homeward(shard, shard).wait_recv()
-
-        for shard in range(count):
-
-            @pl.when(me != shard)
-            def _():
-                outward(shard, me).wait_send()
-                homeward(shard, me).wait_send()
-
-        dev_ref[...] = back[...]
+                homeward(shard, mine).wait_send()
+
+        for j in range(each):
+            dev_ref[j] = back[count - each + j]
 
 
 def finish_kernel(
-    span, x_ref, g_ref, b_ref, c_ref, e_ref, f_ref, dev_ref, yp_ref, dxp_ref, dwp_ref, drp_ref, y_ref, dx_ref, dw_ref, dr_ref
+    span, done, x_ref, g_ref, b_ref, c_ref, e_ref, f_ref, dev_ref, yp_ref, dxp_ref, dwp_ref, drp_ref, y_ref, dx_ref, dw_ref, dr_ref
 ):
-    spread = head_spread_halves(e_ref.shape[1] // 2, pl.program_id(0) * span, span * HEAD_DIM)
-    e_wide = dot_nn(e_ref[...], spread)
-    f_wide = dot_nn(f_ref[...], spread)
-    grad_in = (e_wide * g_ref[...].astype(F32)).astype(BF16)
-    data_in = (f_wide * x_ref[...].astype(F32)).astype(BF16)
-    parts = range(dev_ref.shape[0])
-    state = jnp.concatenate([dev_ref[j, :STATE, :] for j in parts], axis=1)
-    grad = jnp.concatenate([dev_ref[j, STATE:, :] for j in parts], axis=1)
-    y_ref[...] = (yp_ref[...].astype(F32) + e_wide * dot_nn(c_ref[...], state)).astype(BF16)
-    dx_ref[...] = (dxp_ref[...].astype(F32) + f_wide * dot_nn(b_ref[...], grad)).astype(BF16)
-    dw_ref[...] = dwp_ref[...] + dot_nt(data_in, grad)
-    dr_ref[...] = drp_ref[...] + dot_nt(grad_in, state)
+    group = pl.program_id(0)
+
+    @pl.when(group < done)
+    def _():
+        y_ref[...] = yp_ref[...]
+        dx_ref[...] = dxp_ref[...]
+        dw_ref[...] = dwp_ref[...]
+        dr_ref[...] = drp_ref[...]
+
+    @pl.when(group >= done)
+    def _():
+        spread = head_spread_halves(e_ref.shape[1] // 2, group * span, span * HEAD_DIM)
+        e_wide = dot_nn(e_ref[...], spread)
+        f_wide = dot_nn(f_ref[...], spread)
+        grad_in = (e_wide * g_ref[...].astype(F32)).astype(BF16)
+        data_in = (f_wide * x_ref[...].astype(F32)).astype(BF16)
+        parts = range(dev_ref.shape[0])
+        state = jnp.concatenate([dev_ref[j, :STATE, :] for j in parts], axis=1)
+        grad = jnp.concatenate([dev_ref[j, STATE:, :] for j in parts], axis=1)
+        y_ref[...] = (yp_ref[...].astype(F32) + e_wide * dot_nn(c_ref[...], state)).astype(BF16)
+        dx_ref[...] = (dxp_ref[...].astype(F32) + f_wide * dot_nn(b_ref[...], grad)).astype(BF16)
+        dw_ref[...] = dwp_ref[...] + dot_nt(data_in, grad)
+        dr_ref[...] = drp_ref[...] + dot_nt(grad_in, state)
 
 
 def on_device(
@@ -499,12 +549,14 @@
     tables = [whole_spec((heads, tokens)), whole_spec((1, heads))]
     if chunks == seq_count:
 
+        done = groups - 1
+
         def served(i):
-            return owner_at(jnp.minimum(i, chunks - 1), chunks)
+            return jnp.minimum(i, chunks - 1)
 
         def block_of(i):
             place = jnp.clip(i - chunks, 0, groups * blocks - 1)
-            return (lax.rem(place, blocks), place // blocks)
+            return (lax.rem(place, blocks), lax.rem(place // blocks + groups - 1, groups))
 
         whole_e, whole_f, device, *parts = pl.pallas_call(
             functools.partial(exchange_kernel, blocks, span, groups, seq_count),
@@ -512,14 +564,14 @@
             out_shape=(
                 column_shape,
                 column_shape,
-                jax.ShapeDtypeStruct((chunks, 2 * STATE, CHUNK), BF16),
+                jax.ShapeDtypeStruct((group_chunks, 2 * STATE, CHUNK), BF16),
                 *part_shapes,
             ),
             in_specs=[smem, smem, *chunk_specs(served), *tables, whole_spec((1, heads)), *part_specs(block_of)],
             out_specs=(
                 whole_spec((tokens, 2 * heads)),
                 whole_spec((tokens, 2 * heads)),
-                whole_spec((chunks, 2 * STATE, CHUNK)),
+                whole_spec((group_chunks, 2 * STATE, CHUNK)),
                 *part_specs(block_of),
             ),
             scratch_shapes=[
@@ -527,6 +579,7 @@
                 pltpu.VMEM((tokens, 2 * heads), BF16),
                 pltpu.VMEM((blocks, STATE, channels), BF16),
                 pltpu.VMEM((blocks, STATE, channels), BF16),
+                pltpu.VMEM((blocks, 16, channels), F32),
                 pltpu.VMEM((chunks, rows, CHUNK), BF16),
                 pltpu.VMEM((chunks, rows, CHUNK), BF16),
                 pltpu.VMEM((chunks, 2 * STATE, CHUNK), BF16),
@@ -557,6 +610,7 @@
             own_read,
         )
     else:
+        done = 0
         state_shape = jax.ShapeDtypeStruct((blocks, STATE, channels), BF16)
         message, pre, suf, e_cols, f_cols, whole_e, whole_f = pl.pallas_call(
             functools.partial(summary_kernel, blocks),
@@ -574,6 +628,7 @@
                 pl.BlockSpec((blocks, STATE, CHUNK), lambda i: (0, 0, i)),
                 *[whole_spec((tokens, 2 * heads))] * 4,
             ),
+            scratch_shapes=[pltpu.VMEM((blocks, 16, CHUNK), F32)],
             compiler_params=params,
             name="summary",
         )(doc_start, seq_input, out_grad, own_write, own_read, step_size, rate_row)
@@ -613,15 +668,21 @@
         device = jnp.transpose(device, (1, 0, 2)).reshape(2 * STATE, chunks, CHUNK)
         device = jnp.transpose(device, (1, 0, 2))
 
+    def by_open_block(g, k):
+        return (jnp.where(g < done, 0, k), jnp.maximum(g, done))
+
+    def open_rows(g, k):
+        return (jnp.where(g < done, 0, k), 0)
+
     mixed, input_grad, write_sum, read_sum = pl.pallas_call(
-        functools.partial(finish_kernel, span),
+        functools.partial(finish_kernel, span, done),
         grid=(groups, blocks),
         out_shape=part_shapes,
         in_specs=[
-            *part_specs(by_block),
-            pl.BlockSpec((BLOCK, 2 * heads), lambda g, k: (k, 0)),
-            pl.BlockSpec((BLOCK, 2 * heads), lambda g, k: (k, 0)),
-            pl.BlockSpec((group_chunks, 2 * STATE, CHUNK), lambda g, k: (g, 0, 0)),
+            *part_specs(by_open_block),
+            pl.BlockSpec((BLOCK, 2 * heads), open_rows),
+            pl.BlockSpec((BLOCK, 2 * heads), open_rows),
+            pl.BlockSpec((group_chunks, 2 * STATE, CHUNK), lambda g, k: (jnp.maximum(g - done, 0), 0, 0)),
             *part_specs(by_block),
         ],
         out_specs=part_specs(by_block),

time: 73.4 us -> 81.7 us (1.11)
  the two profiles are of different devices: /device:TPU:17 before, /device:TPU:21 now
where the time goes in v3:
time: 81.7 us; the launch traced here: 81.4 us
  Pallas kernels  80.8 us (99%)
    pallas_call x1, Pallas kernels, on_device(): pl.pallas_call(functools.partial(exchange_kernel, blocks, span, groups, s...  67.6 us
    pallas_call x1, Pallas kernels, on_device(): pl.pallas_call(functools.partial(finish_kernel, span, done), grid=(groups...  13.2 us

profile of v3, /device:TPU:21, one launch (start us, length us, event | category | flops | bytes accessed | tf_op | source)
XLA Modules:
  0.0 81.4 jit_solution(16948503148713647171)
XLA Ops:
  0.6 67.6 %exchange.1 = (bf16[1024,64]{1,0:T(8,128)(2,1)}, bf16[1024,64]{1,0:T(8,128)(2,1)}, bf16[4,256,256]{2,1,0:T(8,128)(2,1)}, bf16[1024,2048]{1,0:T(8,128)(2,1)}, bf1...) custom-call(s32[32]{0:T(128)} %doc_ref.1, s32[8]{0:T(128)} %place_ref.1, ...), custom_call_target="tpu_custom_call" | custom-call | tf_op jit(solution)/shard_map/exchange/pallas_call | solution.py:561
  68.2 13.2 %finish.1 = (bf16[1024,2048]{1,0:T(8,128)(2,1)}, bf16[1024,2048]{1,0:T(8,128)(2,1)}, f32[1024,256]{1,0:T(8,128)}, f32[1024,256]{1,0:T(8,128)}) custom-call(bf16[1024,2048]{1,0:T(8,128)(2,1)} %x_ref.3, bf16[1024,2048]{1,0:T(8,128)(2,1)} %g_ref.3, bf16[1024,256]{1,0:T(8,128)(2,1)} %b_ref.3, bf16[1024,256]{1,0:T(8,128)(2,1)} %c_ref.3, ...), custom_call_target="tpu_custom_call" | custom-call | tf_op jit(solution)/shard_map/finish/pallas_call | solution.py:677

commit v4 on v2

--- a/solution.py
+++ b/solution.py
@@ -14,7 +14,8 @@
 BLOCK = 256
 CHUNK = 256
 EXTRA = 16
-VMEM_LIMIT = 60 * 1024 * 1024
+VMEM_LIMIT = 34 * 1024 * 1024
+FINISH_LIMIT = 16 * 1024 * 1024
 
 F32 = jnp.float32
 BF16 = jnp.bfloat16
@@ -352,8 +353,7 @@
 
     half = count // 2
     turn = 2 * lax.rem(me, half) + me // half
-    early = half + 1
-    chain_step = early + (turn * (steps - 1 - early)) // (count - 1)
+    chain_step = count + (turn * (groups * blocks * 5 // 8)) // (count - 1)
 
     @pl.when(step == chain_step)
     def _():
@@ -625,7 +625,7 @@
             *part_specs(by_block),
         ],
         out_specs=part_specs(by_block),
-        compiler_params=params,
+        compiler_params=pltpu.CompilerParams(vmem_limit_bytes=FINISH_LIMIT),
         name="finish",
     )(seq_input, out_grad, own_write, own_read, whole_e, whole_f, device, *parts)
 

time: 73.4 us -> 73.1 us (level)
  the two profiles are of different devices: /device:TPU:17 before, /device:TPU:29 now
where the time goes in v4:
time: 73.1 us; the launch traced here: 72.8 us
  Pallas kernels  64.4 us (88%)
  local copies, waits for them, and re-layouts  7.79 us (11%)
    pallas_call x1, Pallas kernels, on_device(): pl.pallas_call(functools.partial(exchange_kernel, blocks, span, groups, s...  53.7 us
    pallas_call x1, Pallas kernels, on_device(): pl.pallas_call(functools.partial(finish_kernel, span), grid=(groups, bloc...  10.6 us
    unnamed x20, local copies, waits for them, and re-layouts  7.79 us

profile of v4, /device:TPU:29, one launch (start us, length us, event | category | flops | bytes accessed | tf_op | source)
XLA Modules:
  0.0 72.8 jit_solution(11211217114307038292)
XLA Ops:
  0.6 0.0 copy-start
  0.6 2.2 %copy-done = bf16[1024,2048]{1,0:T(8,128)(2,1)S(1)} copy-done((bf16[1024,2048]{1,0:T(8,128)(2,1)S(1)}, bf16[1024,2048]{1,0:T(8,128)(2,1)}, u32[]{:S(2)}) %copy-start) | copy-done | bytes 4194328
  2.8 0.0 copy-start.3
  2.8 1.0 %copy-done.3 = bf16[1024,256]{1,0:T(8,128)(2,1)S(1)} copy-done((bf16[1024,256]{1,0:T(8,128)(2,1)S(1)}, bf16[1024,256]{1,0:T(8,128)(2,1)}, u32[]{:S(2)}) %copy-start.3) | copy-done | bytes 524312
  3.9 0.0 copy-start.4
  3.9 1.0 %copy-done.4 = bf16[1024,256]{1,0:T(8,128)(2,1)S(1)} copy-done((bf16[1024,256]{1,0:T(8,128)(2,1)S(1)}, bf16[1024,256]{1,0:T(8,128)(2,1)}, u32[]{:S(2)}) %copy-start.4) | copy-done | bytes 524312
  4.9 0.0 copy-start.5
  4.9 0.9 %copy-done.5 = f32[32,1024]{1,0:T(8,128)S(1)} copy-done((f32[32,1024]{1,0:T(8,128)S(1)}, f32[32,1024]{1,0:T(8,128)}, u32[]{:S(2)}) %copy-start.5) | copy-done | bytes 131096
  5.8 0.0 copy-start.6
  5.8 0.7 copy-done.6
  6.5 0.0 copy-start.7
  6.5 0.7 copy-done.7
  7.1 0.0 copy-start.8
  7.1 0.7 copy-done.8
  7.8 0.0 copy-start.9
  7.8 0.7 copy-done.9
  8.4 0.0 copy-start.1
  8.4 0.0 copy-start.2
  8.4 53.7 %exchange.1 = (bf16[1024,64]{1,0:T(8,128)(2,1)S(1)}, bf16[1024,64]{1,0:T(8,128)(2,1)S(1)}, bf16[8,256,256]{2,1,0:T(8,128)(2,1)S(1)}, bf16[1024,2048]{1,0:T(8,128...) custom-call(s32[32]{0:T(128)S(1)} %copy-done.6, s32[8]{0:T(128)S(1)} %copy-done.7, ...), custom_call_target="tpu_custom_call" | custom-call | tf_op jit(solution)/shard_map/exchange/pallas_call | solution.py:509
  62.2 0.0 copy-done.1
  62.2 0.0 copy-done.2
  62.2 10.6 %finish.1 = (bf16[1024,2048]{1,0:T(8,128)(2,1)}, bf16[1024,2048]{1,0:T(8,128)(2,1)}, f32[1024,256]{1,0:T(8,128)}, f32[1024,256]{1,0:T(8,128)}) custom-call(bf16[1024,2048]{1,0:T(8,128)(2,1)S(1)} %copy-done.1, bf16[1024,2048]{1,0:T(8,128)(2,1)S(1)} %copy-done.2, bf16[1024,256]{1,0:T(8,128)(2,1)S(1)} %copy-done.3, bf16[1024,256]{1,0:T(8,128)(2,1)S(1)} %copy-done.4, ...), custom_call_target="tpu_custom_call" | custom-call | tf_op jit(solution)/shard_map/finish/pallas_call | solution.py:616
Async XLA Ops:
  0.6 2.2 %copy-start = (bf16[1024,2048]{1,0:T(8,128)(2,1)S(1)}, bf16[1024,2048]{1,0:T(8,128)(2,1)}, u32[]{:S(2)}) copy-start(bf16[1024,2048]{1,0:T(8,128)(2,1)} %x_ref.3) | copy-start | bytes 12582916
  2.8 1.0 %copy-start.3 = (bf16[1024,256]{1,0:T(8,128)(2,1)S(1)}, bf16[1024,256]{1,0:T(8,128)(2,1)}, u32[]{:S(2)}) copy-start(bf16[1024,256]{1,0:T(8,128)(2,1)} %b_ref.3) | copy-start | bytes 1572868
  3.9 1.0 %copy-start.4 = (bf16[1024,256]{1,0:T(8,128)(2,1)S(1)}, bf16[1024,256]{1,0:T(8,128)(2,1)}, u32[]{:S(2)}) copy-start(bf16[1024,256]{1,0:T(8,128)(2,1)} %c_ref.3) | copy-start | bytes 1572868
  4.9 0.9 %copy-start.5 = (f32[32,1024]{1,0:T(8,128)S(1)}, f32[32,1024]{1,0:T(8,128)}, u32[]{:S(2)}) copy-start(f32[32,1024]{1,0:T(8,128)} %step_ref.1) | copy-start | bytes 393220
  5.8 0.7 copy-start.6
  6.5 0.7 copy-start.7
  7.1 0.7 copy-start.8
  7.8 0.7 copy-start.9
  8.4 53.7 %copy-start.1 = (bf16[1024,2048]{1,0:T(8,128)(2,1)S(1)}, bf16[1024,2048]{1,0:T(8,128)(2,1)}, u32[]{:S(2)}) copy-start(bf16[1024,2048]{1,0:T(8,128)(2,1)} %x_ref.3) | copy-start | bytes 12582916
  8.4 53.7 %copy-start.2 = (bf16[1024,2048]{1,0:T(8,128)(2,1)S(1)}, bf16[1024,2048]{1,0:T(8,128)(2,1)}, u32[]{:S(2)}) copy-start(bf16[1024,2048]{1,0:T(8,128)(2,1)} %g_ref.3) | copy-start | bytes 12582916

commit v5 on v4

--- a/solution.py
+++ b/solution.py
@@ -14,8 +14,8 @@
 BLOCK = 256
 CHUNK = 256
 EXTRA = 16
-VMEM_LIMIT = 34 * 1024 * 1024
-FINISH_LIMIT = 16 * 1024 * 1024
+VMEM_LIMIT = 60 * 1024 * 1024
+FINISH_LIMIT = 60 * 1024 * 1024
 
 F32 = jnp.float32
 BF16 = jnp.bfloat16

time: 73.1 us -> 71.4 us (0.977)
  local copies, waits for them, and re-layouts: 7.79 us -> 0 us
  Pallas kernels: 64.4 us -> 70.5 us
    unnamed x20 -> x0, local copies, waits for them, and re-layouts: 7.79 us -> none
    pallas_call x1, Pallas kernels: 10.6 us -> 14.8 us  [on_device(): pl.pallas_call(functools.partial(finish_kernel, span), grid=(groups, bloc...]
    pallas_call x1, Pallas kernels: 53.7 us -> 55.7 us  [on_device(): pl.pallas_call(functools.partial(exchange_kernel, blocks, span, groups, s...]
where the time goes in v5:
time: 71.4 us; the launch traced here: 71.1 us
  Pallas kernels  70.5 us (99%)
    pallas_call x1, Pallas kernels, on_device(): pl.pallas_call(functools.partial(exchange_kernel, blocks, span, groups, s...  55.7 us
    pallas_call x1, Pallas kernels, on_device(): pl.pallas_call(functools.partial(finish_kernel, span), grid=(groups, bloc...  14.8 us

profile of v5, /device:TPU:29, one launch (start us, length us, event | category | flops | bytes accessed | tf_op | source)
XLA Modules:
  0.0 71.1 jit_solution(1617423030884459236)
XLA Ops:
  0.6 55.7 %exchange.1 = (bf16[1024,64]{1,0:T(8,128)(2,1)}, bf16[1024,64]{1,0:T(8,128)(2,1)}, bf16[8,256,256]{2,1,0:T(8,128)(2,1)}, bf16[1024,2048]{1,0:T(8,128)(2,1)}, bf1...) custom-call(s32[32]{0:T(128)} %doc_ref.1, s32[8]{0:T(128)} %place_ref.1, ...), custom_call_target="tpu_custom_call" | custom-call | tf_op jit(solution)/shard_map/exchange/pallas_call | solution.py:509
  56.3 14.8 %finish.1 = (bf16[1024,2048]{1,0:T(8,128)(2,1)}, bf16[1024,2048]{1,0:T(8,128)(2,1)}, f32[1024,256]{1,0:T(8,128)}, f32[1024,256]{1,0:T(8,128)}) custom-call(bf16[1024,2048]{1,0:T(8,128)(2,1)} %x_ref.3, bf16[1024,2048]{1,0:T(8,128)(2,1)} %g_ref.3, bf16[1024,256]{1,0:T(8,128)(2,1)} %b_ref.3, bf16[1024,256]{1,0:T(8,128)(2,1)} %c_ref.3, ...), custom_call_target="tpu_custom_call" | custom-call | tf_op jit(solution)/shard_map/finish/pallas_call | solution.py:616
